TPU v7x, 32 devices: a whole 2x2x4 slice. The times are simulated.
32 devices in a mesh: section: 4 (over z), expert: 8 (over y, x, core).
Axes of the slice: x: 2, y: 2, z: 4, core: 2. Of those that a mesh axis runs over, the one named last changes fastest.
Arguments:
- fwd_sent: bfloat16 [4, 512, 4096], P('section', 'expert'), may hold values from -6 to 6
- bwd_sent: bfloat16 [4, 512, 4096], P('section', 'expert'), may hold values from -6 to 6
- bwd_saved: bfloat16 [4, 512, 4096], P('section', 'expert'), may hold values from -6 to 6
- fwd_routes: int32 [4, 512, 8], P('section', 'expert'), may hold values from 0 to 127, all different within a row; in each aligned block of 64 rows (0 to 63, 64 to 127, ..., all dimensions but the last counted through in order) at most 8 rows name the same one
- bwd_routes: int32 [4, 512, 8], P('section', 'expert'), may hold values from 0 to 127, all different within a row; in each aligned block of 64 rows (0 to 63, 64 to 127, ..., all dimensions but the last counted through in order) at most 8 rows name the same one
- fwd_logits: float32 [4, 512, 128], P('section', 'expert'), may hold values from -3 to 330
- bwd_logits: float32 [4, 512, 128], P('section', 'expert'), may hold values from -3 to 330
- norm_gain: bfloat16 [4, 4096], P('section'), may hold values from 0.5 to 1.5
- w_gate: bfloat16 [4, 4096, 3072], P('section', None, 'expert'), may hold values from -0.09375 to 0.09375
- w_up: bfloat16 [4, 4096, 3072], P('section', None, 'expert'), may hold values from -0.09375 to 0.09375
- w_down: bfloat16 [4, 3072, 4096], P('section', 'expert'), may hold values from -0.4375 to 0.4375
Outputs:
- fwd_out: bfloat16 [4, 512, 4096], P('section', 'expert')
- bwd_out: bfloat16 [4, 512, 4096], P('section', 'expert')
- balance: float32 [4, 128], P('section')
Inputs may be any that keep to these rules, and one draw needn't show every extreme that they name: `fwd_routes`: each token names 8 different experts; among the 64 tokens of one index of expert no expert is named more than 8 times, a bound that some block reaches. `bwd_routes`: as for fwd_routes.
All inputs are finite; a program needn't handle non-finite values.
Results may differ from a plain program's by a relative error of at most 0.0045.
Values may be sent and summed in bfloat16 or wider, within the bound.
A program may use at most 64 MiB of HBM per device.

v0:
```python
import jax
import jax.numpy as jnp
from jax import lax
from jax.sharding import PartitionSpec as P

EXPERTS = 128
TOPK = 8
EXP_WIN = 2
CAP = 8


epsilon = 1e-06
exact = lax.Precision.HIGHEST


def from_behind(block, axis, distance):
    devices = range(lax.axis_size(axis))
    route = [((i - distance) % len(devices), i) for i in devices]
    return lax.ppermute(block, axis, route)


def norm_rows(values, gain_row):
    widened = values.astype(jnp.float32)
    inverse = lax.rsqrt(jnp.mean(widened * widened, axis=-1, keepdims=True) + epsilon)
    normed = (widened * inverse * gain_row.astype(jnp.float32)).astype(jnp.bfloat16)
    return (normed, widened, inverse)


def slot_tables(routes, logits):
    tokens_here = routes.shape[0]
    expert_ids = jnp.arange(logits.shape[1], dtype=jnp.int32)
    chosen = jnp.sum(
        jnp.where(routes[:, :, None] == expert_ids[None, None, :], logits[:, None, :], 0.0), axis=2
    )
    gates = jax.nn.softmax(chosen, axis=1)
    match = (routes[:, :, None] == jnp.arange(EXP_WIN, dtype=jnp.int32)[None, None, :]).astype(
        jnp.int32
    )
    flat = match.reshape(tokens_here * TOPK, EXP_WIN)
    earlier = (jnp.cumsum(flat, axis=0) - flat).reshape(tokens_here, TOPK, EXP_WIN)
    placed = match[..., None] * (earlier[..., None] == jnp.arange(CAP, dtype=jnp.int32)).astype(
        jnp.int32
    )
    select = jnp.sum(placed, axis=1).astype(jnp.float32)
    gate_slot = jnp.sum(placed.astype(jnp.float32) * gates[:, :, None, None], axis=(0, 1))
    return (select, gate_slot)


def usage_terms(routes, logits):
    expert_ids = jnp.arange(logits.shape[1], dtype=jnp.int32)
    counts = jnp.sum(
        (routes[:, :, None] == expert_ids[None, None, :]).astype(jnp.float32), axis=(0, 1)
    )
    prob_sums = jnp.sum(jax.nn.softmax(logits, axis=1), axis=0)
    return (counts, prob_sums)


def spread_rows(slot_rows, devices):
    held, slots, width = slot_rows.shape
    return jnp.broadcast_to(slot_rows[:, None], (held, devices // held, slots, width)).reshape(
        devices, slots, width
    )


def combine_parts(returned):
    devices, slots, width = returned.shape
    return jnp.sum(
        returned.astype(jnp.float32).reshape(EXP_WIN, devices // EXP_WIN, slots, width), axis=1
    )


def expert_forward(arrived, gate_slab, up_slab, down_slab):
    layout = arrived.shape
    flat = arrived.reshape(-1, layout[-1])
    gate_pre = jnp.dot(flat, gate_slab, preferred_element_type=jnp.float32)
    up_pre = jnp.dot(flat, up_slab, preferred_element_type=jnp.float32)
    hidden = (jax.nn.silu(gate_pre) * up_pre).astype(jnp.bfloat16)
    result = jnp.dot(hidden, down_slab, preferred_element_type=jnp.float32).astype(jnp.bfloat16)
    return result.reshape(layout)


def expert_backward(arrived, arrived_grads, gate_slab, up_slab, down_slab):
    layout = arrived.shape
    flat = arrived.reshape(-1, layout[-1])
    grad_flat = arrived_grads.reshape(-1, layout[-1])
    gate_pre = jnp.dot(flat, gate_slab, preferred_element_type=jnp.float32)
    up_pre = jnp.dot(flat, up_slab, preferred_element_type=jnp.float32)
    sigma = jax.nn.sigmoid(gate_pre)
    contract = (((1,), (1,)), ((), ()))
    d_hidden = lax.dot_general(grad_flat, down_slab, contract, preferred_element_type=jnp.float32)
    d_gate = (d_hidden * up_pre * sigma * (1.0 + gate_pre * (1.0 - sigma))).astype(jnp.bfloat16)
    d_up = (d_hidden * gate_pre * sigma).astype(jnp.bfloat16)
    result = lax.dot_general(d_gate, gate_slab, contract, preferred_element_type=jnp.float32)
    result = result + lax.dot_general(d_up, up_slab, contract, preferred_element_type=jnp.float32)
    return result.astype(jnp.bfloat16).reshape(layout)


def body(
    fwd_sent,
    bwd_sent,
    bwd_saved,
    fwd_routes,
    bwd_routes,
    fwd_logits,
    bwd_logits,
    norm_gain,
    w_gate,
    w_up,
    w_down,
):
    devices = lax.axis_size("expert")
    gain_row = norm_gain[0]
    gate_slab = w_gate[0]
    up_slab = w_up[0]
    down_slab = w_down[0]
    x_in = from_behind(fwd_sent[0], "section", 1)
    upstream = from_behind(bwd_sent[0], "section", -1)
    normed = norm_rows(x_in, gain_row)[0]
    fwd_select, fwd_gates = slot_tables(fwd_routes[0], fwd_logits[0])
    fwd_rows = jnp.einsum(
        "tec,td->ecd", fwd_select.astype(jnp.bfloat16), normed, preferred_element_type=jnp.float32
    ).astype(jnp.bfloat16)
    fwd_send = spread_rows(fwd_rows, devices)
    saved_normed, saved_wide, saved_inverse = norm_rows(bwd_saved[0], gain_row)
    bwd_select, bwd_gates = slot_tables(bwd_routes[0], bwd_logits[0])
    bwd_onehot = bwd_select.astype(jnp.bfloat16)
    saved_rows = jnp.einsum(
        "tec,td->ecd", bwd_onehot, saved_normed, preferred_element_type=jnp.float32
    ).astype(jnp.bfloat16)
    grad_rows = jnp.einsum("tec,td->ecd", bwd_onehot, upstream, preferred_element_type=jnp.float32)
    grad_rows = (grad_rows * bwd_gates[:, :, None]).astype(jnp.bfloat16)
    saved_send = spread_rows(saved_rows, devices)
    grad_send = spread_rows(grad_rows, devices)
    counts, prob_sums = usage_terms(fwd_routes[0], fwd_logits[0])
    counts, prob_sums = lax.psum((counts, prob_sums), "expert")
    fwd_parts = lax.all_to_all(
        expert_forward(
            lax.all_to_all(fwd_send, "expert", split_axis=0, concat_axis=0, tiled=True),
            gate_slab,
            up_slab,
            down_slab,
        ),
        "expert",
        split_axis=0,
        concat_axis=0,
        tiled=True,
    )
    bwd_parts = lax.all_to_all(
        expert_backward(
            lax.all_to_all(saved_send, "expert", split_axis=0, concat_axis=0, tiled=True),
            lax.all_to_all(grad_send, "expert", split_axis=0, concat_axis=0, tiled=True),
            gate_slab,
            up_slab,
            down_slab,
        ),
        "expert",
        split_axis=0,
        concat_axis=0,
        tiled=True,
    )
    fwd_expert = combine_parts(fwd_parts)
    mixed = jnp.einsum("tec,ecd->td", fwd_select * fwd_gates[None], fwd_expert, precision=exact)
    fwd_out = (x_in.astype(jnp.float32) + mixed).astype(jnp.bfloat16)
    back_expert = combine_parts(bwd_parts)
    d_normed = jnp.einsum("tec,ecd->td", bwd_select, back_expert, precision=exact)
    weighted = gain_row.astype(jnp.float32) * d_normed
    d_saved = saved_inverse * weighted - saved_wide * saved_inverse**3 * jnp.mean(
        saved_wide * weighted, axis=-1, keepdims=True
    )
    bwd_out = (upstream.astype(jnp.float32) + d_saved).astype(jnp.bfloat16)
    tokens_all = fwd_routes.shape[1] * devices
    balance = EXPERTS * (counts / (tokens_all * TOPK)) * (prob_sums / tokens_all)
    return (fwd_out[None], bwd_out[None], balance[None])


def solution(mesh):
    return jax.shard_map(
        body,
        mesh=mesh,
        in_specs=(
            P("section", "expert", None),
            P("section", "expert", None),
            P("section", "expert", None),
            P("section", "expert", None),
            P("section", "expert", None),
            P("section", "expert", None),
            P("section", "expert", None),
            P("section", None),
            P("section", None, "expert"),
            P("section", None, "expert"),
            P("section", "expert", None),
        ),
        out_specs=(P("section", "expert", None), P("section", "expert", None), P("section", None)),
        check_vma=False,
    )
```

profile of v0, /device:TPU:0, one launch (start us, length us, event | category | flops | bytes accessed | tf_op | source)
XLA Modules:
  0.0 105.5 jit_solution(2052434266057660180)
XLA Ops:
  0.7 5.1 %collective-permute-start.1 = (bf16[64,4096]{1,0:T(8,128)(2,1)}, bf16[64,4096]{1,0:T(8,128)(2,1)}, u32[]{:S(2)}, u32[]{:S(2)}) collective-permute-start(bf16[64,4096]{1,0:T(8,128)(2,1)} %bitcast.150), channel_id=1, source_target_pairs={{8,0},{16,8},{24,16},{0,24},{9,1},{17,9},{25,17},{1,25},{10,2},{18... | collective-permute-start | bytes 1572872 | tf_op jit(solution)/shard_map/ppermute | solution.py:19
  5.8 0.8 copy.50
  6.6 0.1 eq.158
  6.7 0.1 eq.162
  6.8 0.6 reduce-window.16
  7.4 0.2 slice_reduce_fusion
  7.6 0.2 reduce-window.19
  7.8 0.1 add_bitcast_fusion
  7.9 0.1 eq.166
  8.0 0.1 copy.52
  8.0 0.7 compare_convert_fusion
  8.7 0.7 mul.195
  9.5 1.2 %fusion.43 = f32[64]{0:T(128)S(1)} fusion(bf16[1,64,4096]{2,1,0:T(8,128)(2,1)} %param.13), kind=kLoop, calls=%fused_computation.44 | loop fusion | flops 786368 | bytes 524544 | tf_op jit(solution)/shard_map/reduce_sum | solution.py:24
  10.8 1.3 %convolution_convert_fusion.1 = bf16[2,8,4096]{2,1,0:T(8,128)(2,1)S(1)} fusion(bf16[1,64,4096]{2,1,0:T(8,128)(2,1)} %param.13, f32[64]{0:T(128)S(1)} %get-tuple-element.8, f32[4096]{0:T(1024)S(1)} %bitcast.140, s32[64,2,8]{0,2,1:T(8,128)S(1)} %select_reduce_fusion.2), kind=kOutput, calls=%fused_computation.13 | convolution fusion | flops 9504768 | bytes 676096 | tf_op jit(solution)/shard_map/tec,td->ecd/dot_general | solution.py:127
  12.1 0.8 broadcast_in_dim.42
  12.9 4.1 %all-to-all-start.3 = ((bf16[8,8,4096]{2,1,0:T(8,128)(2,1)}), bf16[8,8,4096]{2,1,0:T(8,128)(2,1)}, u32[]{:S(2)}, u32[]{:S(2)}) async-start(bf16[8,8,4096]{2,1,0:T(8,128)(2,1)} %bitcast.136), calls=%async_computation.3 | async-start | bytes 1048576 | tf_op jit(solution)/shard_map/all_to_all | solution.py:150
  17.1 0.1 collective-permute-start
  17.2 0.1 copy.53
  17.3 0.1 copy.44
  17.3 0.1 eq.139
  17.4 0.1 eq.143
  17.5 0.1 copy.47
  17.6 0.2 select_reduce_fusion
  17.9 0.1 copy.55
  17.9 0.1 reduce_max.28
  18.0 0.2 convert_reduce_fusion.2
  18.3 0.1 copy.49
  18.3 0.1 reduce_max.27
  18.5 0.1 reduce_max.29
  18.6 0.6 reduce-window.14
  19.2 0.2 slice_reduce_fusion.1
  19.5 0.2 reduce-window.15
  19.6 0.1 add_bitcast_fusion.1
  19.7 0.1 eq.147
  19.8 0.1 copy.46
  19.9 0.2 fusion.88
  20.1 0.1 divide_reduce_fusion
  20.3 15.1 %all-reduce = (f32[128]{0:T(128)S(1)}, f32[128]{0:T(128)S(1)}) all-reduce(f32[128]{0:T(128)S(1)} %divide_reduce_fusion, f32[128]{0:T(128)S(1)} %get-tuple-element.3), channel_id=1, replica_groups=mesh['section'=4,'expert'=8] {'expert'}, use_global_device_ids=true, to_apply=%region_24.25 | all-reduce | flops 256 | bytes 2048 | tf_op jit(solution)/shard_map/psum | solution.py:135
  35.4 0.1 fusion.84
  35.5 0.1 fusion.82
  35.6 0.5 multiply_bitcast_fusion
  36.1 2.6 %fusion.18 = f32[64,384]{1,0:T(8,128)S(1)} fusion(bf16[1,4096,384]{2,1,0:T(8,128)(2,1)} %param.19, bf16[8,8,4096]{2,1,0:T(8,128)(2,1)} %all-to-all-done.3), kind=kOutput, calls=%fused_computation.25 | convolution fusion | flops 201326592 | bytes 3768320 | tf_op jit(solution)/shard_map/dot_general | solution.py:86
  38.7 1.2 %fusion.7 = bf16[2,8,4096]{2,1,0:T(8,128)(2,1)S(1)} fusion(bf16[64,4096]{1,0:T(8,128)(2,1)} %collective-permute-done.1, f32[2,8]{1,0:T(2,128)S(1)} %fusion.84, s32[64,2,8]{0,2,1:T(8,128)S(1)} %select_reduce_fusion.2), kind=kOutput, calls=%fused_computation.12 | convolution fusion | flops 8521728 | bytes 659520 | tf_op jit(solution)/shard_map/tec,td->ecd/dot_general | solution.py:130
  40.0 0.8 broadcast_in_dim.41
  40.8 4.1 %all-to-all-start.2 = ((bf16[8,8,4096]{2,1,0:T(8,128)(2,1)}), bf16[8,8,4096]{2,1,0:T(8,128)(2,1)}, u32[]{:S(2)}, u32[]{:S(2)}) async-start(bf16[8,8,4096]{2,1,0:T(8,128)(2,1)} %bitcast.137), calls=%async_computation.2 | async-start | bytes 1048576 | tf_op jit(solution)/shard_map/all_to_all | solution.py:151
  45.0 1.2 %fusion.40 = f32[64]{0:T(128)S(1)} fusion(bf16[64,4096]{1,0:T(8,128)(2,1)} %collective-permute-done), kind=kLoop, calls=%fused_computation.41 | loop fusion | flops 786368 | bytes 524544 | tf_op jit(solution)/shard_map/reduce_sum | solution.py:24
  46.2 1.3 %convolution_convert_fusion.2 = bf16[2,8,4096]{2,1,0:T(8,128)(2,1)S(1)} fusion(bf16[64,4096]{1,0:T(8,128)(2,1)} %collective-permute-done, f32[4096]{0:T(1024)S(1)} %bitcast.141, f32[64]{0:T(128)S(1)} %add_rsqrt_fusion.1, s32[64,2,8]{0,2,1:T(8,128)S(1)} %select_reduce_fusion.3), kind=kOutput, calls=%fused_computation.14 | convolution fusion | flops 9504768 | bytes 676096 | tf_op jit(solution)/shard_map/tec,td->ecd/dot_general | solution.py:120
  47.6 7.1 %all-to-all-done.2 = bf16[8,8,4096]{2,1,0:T(8,128)(2,1)} async-done(((bf16[8,8,4096]{2,1,0:T(8,128)(2,1)}), bf16[8,8,4096]{2,1,0:T(8,128)(2,1)}, u32[]{:S(2)}, u32[]{:S(2)}) %all-to-all-start.2) | async-done | bytes 524320 | tf_op jit(solution)/shard_map/all_to_all | solution.py:151
  54.7 0.8 broadcast_in_dim.37
  55.5 4.1 %all-to-all-start = ((bf16[8,8,4096]{2,1,0:T(8,128)(2,1)}), bf16[8,8,4096]{2,1,0:T(8,128)(2,1)}, u32[]{:S(2)}, u32[]{:S(2)}) async-start(bf16[8,8,4096]{2,1,0:T(8,128)(2,1)} %bitcast.138), calls=%async_computation | async-start | bytes 1048576 | tf_op jit(solution)/shard_map/all_to_all | solution.py:138
  59.7 3.2 %fusion.8 = f32[64,384]{1,0:T(8,128)S(1)} fusion(bf16[1,384,4096]{2,1,0:T(8,128)(2,1)} %param.21, bf16[8,8,4096]{2,1,0:T(8,128)(2,1)} %all-to-all-done.2), kind=kOutput, calls=%fused_computation.15 | convolution fusion | flops 201326592 | bytes 3768320 | tf_op jit(solution)/shard_map/dot_general | solution.py:90
  62.9 4.9 %fusion.16 = f32[64,4096]{1,0:T(8,128)} fusion(bf16[1,4096,384]{2,1,0:T(8,128)(2,1)} %param.19, f32[64,384]{1,0:T(8,128)S(1)} %fusion.8, bf16[1,4096,384]{2,1,0:T(8,128)(2,1)S(1)} %copy-done, bf16[8,8,4096]{2,1,0:T(8,128)(2,1)} %all-to-all-done.3, f32[64,384]{1,0:T(8,128)S(1)} %fusion.18), kind=kOutput, calls=%fused_computation.23 | convolution fusion | flops 402898944 | bytes 8060928 | tf_op jit(solution)/shard_map/dot_general | solution.py:93
  67.8 3.1 %fusion.6 = bf16[8,8,4096]{2,1,0:T(8,128)(2,1)} fusion(f32[64,4096]{1,0:T(8,128)} %fusion.16, bf16[1,4096,384]{2,1,0:T(8,128)(2,1)S(1)} %copy-done, f32[64,384]{1,0:T(8,128)S(1)} %fusion.8, f32[64,384]{1,0:T(8,128)S(1)} %fusion.18), kind=kOutput, calls=%fused_computation.10 | convolution fusion | flops 201998336 | bytes 4915200 | tf_op jit(solution)/shard_map/dot_general | solution.py:94
  70.9 4.1 %all-to-all-start.4 = ((bf16[8,8,4096]{2,1,0:T(8,128)(2,1)}), bf16[8,8,4096]{2,1,0:T(8,128)(2,1)}, u32[]{:S(2)}, u32[]{:S(2)}) async-start(bf16[8,8,4096]{2,1,0:T(8,128)(2,1)} %fusion.6), calls=%async_computation.4 | async-start | bytes 1048576 | tf_op jit(solution)/shard_map/all_to_all | solution.py:148
  75.0 2.6 %fusion.20 = f32[64,384]{1,0:T(8,128)S(1)} fusion(bf16[1,4096,384]{2,1,0:T(8,128)(2,1)} %param.19, bf16[8,8,4096]{2,1,0:T(8,128)(2,1)} %all-to-all-done), kind=kOutput, calls=%fused_computation.27 | convolution fusion | flops 201326592 | bytes 3768320 | tf_op jit(solution)/shard_map/dot_general | solution.py:75
  77.7 4.4 %fusion.4 = bf16[8,8,4096]{2,1,0:T(8,128)(2,1)} fusion(bf16[1,384,4096]{2,1,0:T(8,128)(2,1)} %param.21, bf16[1,4096,384]{2,1,0:T(8,128)(2,1)S(1)} %copy-done, bf16[8,8,4096]{2,1,0:T(8,128)(2,1)} %all-to-all-done, f32[64,384]{1,0:T(8,128)S(1)} %fusion.20), kind=kOutput, calls=%fused_computation.8 | convolution fusion | flops 403062784 | bytes 7438336 | tf_op jit(solution)/shard_map/dot_general | solution.py:78
  82.1 2.8 %all-to-all-done.4 = bf16[8,8,4096]{2,1,0:T(8,128)(2,1)} async-done(((bf16[8,8,4096]{2,1,0:T(8,128)(2,1)}), bf16[8,8,4096]{2,1,0:T(8,128)(2,1)}, u32[]{:S(2)}, u32[]{:S(2)}) %all-to-all-start.4) | async-done | bytes 524320 | tf_op jit(solution)/shard_map/all_to_all | solution.py:148
  84.8 4.1 %all-to-all-start.1 = ((bf16[8,8,4096]{2,1,0:T(8,128)(2,1)}), bf16[8,8,4096]{2,1,0:T(8,128)(2,1)}, u32[]{:S(2)}, u32[]{:S(2)}) async-start(bf16[8,8,4096]{2,1,0:T(8,128)(2,1)} %fusion.4), calls=%async_computation.1 | async-start | bytes 1048576 | tf_op jit(solution)/shard_map/all_to_all | solution.py:136
  89.0 1.1 %convert_reduce_fusion = f32[2,8,4096]{2,1,0:T(8,128)S(1)} fusion(bf16[8,8,4096]{2,1,0:T(8,128)(2,1)} %all-to-all-done.4), kind=kLoop, calls=%fused_computation.52 | loop fusion | flops 458752 | bytes 786432 | tf_op jit(solution)/shard_map/reduce_sum | solution.py:67
  90.1 3.2 %fusion.50 = (f32[64]{0:T(128)S(1)}, f32[64,4096]{1,0:T(8,128)}) fusion(bf16[1,64,4096]{2,1,0:T(8,128)(2,1)} %param.13, f32[2,8,4096]{2,1,0:T(8,128)S(1)} %convert_reduce_fusion, s32[64,2,8]{0,2,1:T(8,128)S(1)} %select_reduce_fusion.2, f32[4096]{0:T(1024)S(1)} %bitcast.142), kind=kOutput, calls=%fused_computation.51 | convolution fusion | flops 51381184 | bytes 1855744 | tf_op jit(solution)/shard_map/tec,ecd->td/dot_general | solution.py:165
  93.4 5.4 %all-to-all-done.1 = bf16[8,8,4096]{2,1,0:T(8,128)(2,1)} async-done(((bf16[8,8,4096]{2,1,0:T(8,128)(2,1)}), bf16[8,8,4096]{2,1,0:T(8,128)(2,1)}, u32[]{:S(2)}, u32[]{:S(2)}) %all-to-all-start.1) | async-done | bytes 524320 | tf_op jit(solution)/shard_map/all_to_all | solution.py:136
  98.7 1.1 %convert_reduce_fusion.1 = f32[2,8,4096]{2,1,0:T(8,128)S(1)} fusion(bf16[8,8,4096]{2,1,0:T(8,128)(2,1)} %all-to-all-done.1), kind=kLoop, calls=%fused_computation.53 | loop fusion | flops 458752 | bytes 786432 | tf_op jit(solution)/shard_map/reduce_sum | solution.py:67
  99.9 2.9 %fusion.5 = bf16[1,64,4096]{2,1,0:T(8,128)(2,1)} fusion(f32[2,8,4096]{2,1,0:T(8,128)S(1)} %convert_reduce_fusion.1, bf16[64,4096]{1,0:T(8,128)(2,1)} %collective-permute-done, s32[64,2,8]{0,2,1:T(8,128)S(1)} %select_reduce_fusion.3, f32[2,8]{1,0:T(2,128)S(1)} %fusion.82), kind=kOutput, calls=%fused_computation.9 | convolution fusion | flops 51120128 | bytes 1314880 | tf_op jit(solution)/shard_map/tec,ecd->td/dot_general | solution.py:162
  102.8 2.6 %fusion.55 = bf16[1,64,4096]{2,1,0:T(8,128)(2,1)} fusion(f32[64,4096]{1,0:T(8,128)} %get-tuple-element.10, bf16[64,4096]{1,0:T(8,128)(2,1)} %collective-permute-done.1, bf16[1,64,4096]{2,1,0:T(8,128)(2,1)} %param.13, f32[64]{0:T(128)S(1)} %broadcast_multiply_fusion, f32[64]{0:T(128)S(1)} %get-tuple-element.7, f32[64]{0:T(128)S(1)} %get-tuple-element.8), kind=kLoop, calls=%fused_computation.54 | loop fusion | flops 2097152 | bytes 2622208 | tf_op jit(solution)/shard_map/broadcast_in_dim | solution.py:173
  (28 shorter events, 0.2 us)
Async XLA Ops:
  0.6 62.2 %copy-start = (bf16[1,4096,384]{2,1,0:T(8,128)(2,1)S(1)}, bf16[1,4096,384]{2,1,0:T(8,128)(2,1)}, u32[]{:S(2)}) copy-start(bf16[1,4096,384]{2,1,0:T(8,128)(2,1)} %param.20) | copy-start | bytes 9437188
  0.6 16.5 %copy-start.2 = (s32[1,64,8]{1,2,0:T(8,128)S(1)}, s32[1,64,8]{1,2,0:T(8,128)}, u32[]{:S(2)}) copy-start(s32[1,64,8]{1,2,0:T(8,128)} %param.15) | copy-start | bytes 6148
  0.7 16.6 %copy-start.3 = (s32[1,64,8]{1,2,0:T(8,128)S(1)}, s32[1,64,8]{1,2,0:T(8,128)}, u32[]{:S(2)}) copy-start(s32[1,64,8]{1,2,0:T(8,128)} %param.14) | copy-start | bytes 6148
  0.7 17.0 %copy-start.4 = (f32[1,64,128]{2,1,0:T(8,128)S(1)}, f32[1,64,128]{2,1,0:T(8,128)}, u32[]{:S(2)}) copy-start(f32[1,64,128]{2,1,0:T(8,128)} %param.17) | copy-start | bytes 98308
  0.7 17.4 %copy-start.1 = (f32[1,64,128]{2,1,0:T(8,128)S(1)}, f32[1,64,128]{2,1,0:T(8,128)}, u32[]{:S(2)}) copy-start(f32[1,64,128]{2,1,0:T(8,128)} %param.16) | copy-start | bytes 98308
  0.7 38.0 %collective-permute-start.1 = (bf16[64,4096]{1,0:T(8,128)(2,1)}, bf16[64,4096]{1,0:T(8,128)(2,1)}, u32[]{:S(2)}, u32[]{:S(2)}) collective-permute-start(bf16[64,4096]{1,0:T(8,128)(2,1)} %bitcast.150), channel_id=1, source_target_pairs={{8,0},{16,8},{24,16},{0,24},{9,1},{17,9},{25,17},{1,25},{10,2},{18... | collective-permute-start | bytes 1572872 | tf_op jit(solution)/shard_map/ppermute | solution.py:19
  12.9 23.1 %all-to-all-start.3 = ((bf16[8,8,4096]{2,1,0:T(8,128)(2,1)}), bf16[8,8,4096]{2,1,0:T(8,128)(2,1)}, u32[]{:S(2)}, u32[]{:S(2)}) async-start(bf16[8,8,4096]{2,1,0:T(8,128)(2,1)} %bitcast.136), calls=%async_computation.3 | async-start | bytes 1048576 | tf_op jit(solution)/shard_map/all_to_all | solution.py:150
  17.1 27.9 %collective-permute-start = (bf16[64,4096]{1,0:T(8,128)(2,1)}, bf16[64,4096]{1,0:T(8,128)(2,1)}, u32[]{:S(2)}, u32[]{:S(2)}) collective-permute-start(bf16[64,4096]{1,0:T(8,128)(2,1)} %bitcast.151), channel_id=1, source_target_pairs={{24,0},{0,8},{8,16},{16,24},{25,1},{1,9},{9,17},{17,25},{26,2},{2,... | collective-permute-start | bytes 1572872 | tf_op jit(solution)/shard_map/ppermute | solution.py:19
  40.8 13.9 %all-to-all-start.2 = ((bf16[8,8,4096]{2,1,0:T(8,128)(2,1)}), bf16[8,8,4096]{2,1,0:T(8,128)(2,1)}, u32[]{:S(2)}, u32[]{:S(2)}) async-start(bf16[8,8,4096]{2,1,0:T(8,128)(2,1)} %bitcast.137), calls=%async_computation.2 | async-start | bytes 1048576 | tf_op jit(solution)/shard_map/all_to_all | solution.py:151
  55.5 15.3 %all-to-all-start = ((bf16[8,8,4096]{2,1,0:T(8,128)(2,1)}), bf16[8,8,4096]{2,1,0:T(8,128)(2,1)}, u32[]{:S(2)}, u32[]{:S(2)}) async-start(bf16[8,8,4096]{2,1,0:T(8,128)(2,1)} %bitcast.138), calls=%async_computation | async-start | bytes 1048576 | tf_op jit(solution)/shard_map/all_to_all | solution.py:138
  70.9 14.0 %all-to-all-start.4 = ((bf16[8,8,4096]{2,1,0:T(8,128)(2,1)}), bf16[8,8,4096]{2,1,0:T(8,128)(2,1)}, u32[]{:S(2)}, u32[]{:S(2)}) async-start(bf16[8,8,4096]{2,1,0:T(8,128)(2,1)} %fusion.6), calls=%async_computation.4 | async-start | bytes 1048576 | tf_op jit(solution)/shard_map/all_to_all | solution.py:148
  84.8 13.9 %all-to-all-start.1 = ((bf16[8,8,4096]{2,1,0:T(8,128)(2,1)}), bf16[8,8,4096]{2,1,0:T(8,128)(2,1)}, u32[]{:S(2)}, u32[]{:S(2)}) async-start(bf16[8,8,4096]{2,1,0:T(8,128)(2,1)} %fusion.4), calls=%async_computation.1 | async-start | bytes 1048576 | tf_op jit(solution)/shard_map/all_to_all | solution.py:136
where the time goes:
time: 107 us; the launch traced here: 105 us
  matrix products  30.9 us (29%)
  starting transfers between devices  25.9 us (24%)
  waiting for transfers between devices  15.3 us (14%)
  blocking collectives  15.1 us (14%)
  other arithmetic  12.5 us (12%)
  local copies, waits for them, and re-layouts  4.78 us (4%)
    psum x1, blocking collectives, body(): counts, prob_sums = lax.psum((counts, prob_sums), 'expert')  15.1 us
    all_to_all x1, waiting for transfers between devices, body(): lax.all_to_all(grad_send, 'expert', split_axis=0, concat_axis=0, tiled=True)  7.13 us
    all_to_all x1, waiting for transfers between devices, body(): lax.all_to_all(expert_forward(lax.all_to_all(fwd_send, 'expert', split_ax...  5.36 us
    ppermute x2, starting transfers between devices, from_behind(): return lax.ppermute(block, axis, route)  5.16 us
    dot_general x1, matrix products, expert_backward(): lax.dot_general(d_gate, gate_slab, contract, preferred_element_type=jnp.f...  4.9 us
    dot_general x1, matrix products, expert_forward(): jnp.dot(hidden, down_slab, preferred_element_type=jnp.float32)  4.38 us
    all_to_all x1, starting transfers between devices, body(): lax.all_to_all(expert_backward(lax.all_to_all(saved_send, 'expert', split...  4.15 us
    all_to_all x1, starting transfers between devices, body(): lax.all_to_all(grad_send, 'expert', split_axis=0, concat_axis=0, tiled=True)  4.14 us
  transfers between devices with their start and end apart: 7, of which 3 were waited for; matrix products, arithmetic and copies ran while one was open for 39% of the time, Pallas kernels for 0%

commit v1 on v0

v1 whole, which is shorter than its diff:
```python
import functools

import jax
import jax.numpy as jnp
from jax import lax
from jax.experimental import pallas as pl
from jax.experimental.pallas import tpu as pltpu
from jax.sharding import PartitionSpec as P

EXPERTS = 128
TOPK = 8
EXP_WIN = 2
CAP = 8
SLOTS = EXP_WIN * CAP
HEAD = 16
CHUNK = 512
EPSILON = 1e-06
MESH = pl.DeviceIdType.MESH
F32 = jnp.float32
BF16 = jnp.bfloat16
NT = (((1,), (1,)), ((), ()))


def iota(shape, dim):
    return lax.broadcasted_iota(jnp.int32, shape, dim)


def dot(a, b):
    return jnp.dot(a, b, preferred_element_type=F32)


def columns(width, body, init=0):
    def step(i, carry):
        return body(pl.ds(pl.multiple_of(i * CHUNK, CHUNK), CHUNK), carry)

    return lax.fori_loop(0, width // CHUNK, step, init)


def route_tables(routes, logits):
    tokens, experts = logits.shape
    lane = iota((tokens, experts), 1)
    chosen = routes[:, 0:1] == lane
    for k in range(1, TOPK):
        chosen = chosen | (routes[:, k : k + 1] == lane)
    hit = chosen.astype(F32)
    top = jnp.max(jnp.where(chosen, logits, -jnp.inf), axis=1, keepdims=True)
    raised = jnp.exp(jnp.where(chosen, logits, top) - top) * hit
    gates = raised / jnp.sum(raised, axis=1, keepdims=True)
    here = jnp.max(jnp.where(lane < EXP_WIN, hit, 0.0), axis=1, keepdims=True)
    marks = jnp.where(lane < EXP_WIN, hit, jnp.where(lane == EXP_WIN, here, 0.0))
    below = (iota((tokens, tokens), 1) < iota((tokens, tokens), 0)).astype(BF16)
    earlier = dot(below, marks.astype(BF16))
    before = earlier[:, EXP_WIN : EXP_WIN + 1]
    count = jnp.sum(here, axis=0, keepdims=True)
    place = jnp.where(
        here > 0.0, before, count + iota((tokens, 1), 0).astype(F32) - before
    )

    def slot_at(slot):
        taken = jnp.zeros(slot.shape, F32)
        gated = jnp.zeros(slot.shape, F32)
        for e in range(EXP_WIN):
            there = (slot // CAP == e) & (
                earlier[:, e : e + 1] == (slot - e * CAP).astype(F32)
            )
            mine = jnp.where(there, hit[:, e : e + 1], 0.0)
            taken = taken + mine
            gated = gated + mine * gates[:, e : e + 1]
        return taken, gated

    taken, gated = slot_at(lane)
    taken = jnp.where(lane < SLOTS, taken, 0.0)
    gated = jnp.where(lane < SLOTS, gated, 0.0)
    taken = jnp.where(lane == SLOTS, place, taken)
    turned = jnp.concatenate([taken, gated], axis=0).T
    select = turned[:SLOTS, :tokens].astype(BF16)
    right = iota((SLOTS, 2 * tokens), 1) >= tokens
    gate_slot = jnp.sum(jnp.where(right, turned[:SLOTS], 0.0), axis=1, keepdims=True)
    place_row = turned[SLOTS : SLOTS + 1]
    again = lane - tokens
    again = jnp.where(again >= SLOTS, again - SLOTS, again)
    back = jnp.where(
        lane < tokens,
        (place == lane.astype(F32)).astype(F32),
        jnp.where(lane < tokens + 2 * SLOTS, slot_at(again)[0], 0.0),
    ).astype(BF16)
    head_select = dot(select, back[:, :HEAD]).astype(BF16)
    return hit, select, head_select, gate_slot, place_row, back[:, : tokens + 2 * SLOTS]


def permutation(place_row, tokens):
    return (iota((tokens, tokens), 0).astype(F32) == place_row[:, :tokens]).astype(BF16)


def halves(rows):
    high = rows.astype(BF16)
    return high, (rows - high.astype(F32)).astype(BF16)


def kernel(
    sections, n,
    fwd_ref, bwd_ref, saved_ref, froute_ref, broute_ref, flogit_ref, blogit_ref, gain_ref,
    wg_hbm, wu_hbm, wd_hbm,
    fout_ref, bout_ref, balance_ref,
    wg, wu, wd, place_out, place_in, head_out, tail_out, head_in, tail_in,
    slab, rx, part, pair_in, summed, home, raw, wide, terms, stats,
    w_sem, z_send, z_recv, d_send, d_recv, f_send, f_recv,
    p_send, p_recv, h_send, h_recv, s_send, s_recv,
):
    tokens, width = fwd_ref.shape
    half = n // 2
    span = half // EXP_WIN
    sec, me = lax.axis_index("section"), lax.axis_index("expert")
    core, mine = lax.rem(me, 2), me // 2
    sibling = me + 1 - 2 * core
    after, ahead = lax.rem(sec + 1, sections), lax.rem(sec + sections - 1, sections)

    loads = [
        pltpu.make_async_copy(src, dst, w_sem.at[i])
        for i, (src, dst) in enumerate(((wg_hbm, wg), (wu_hbm, wu), (wd_hbm, wd)))
    ]
    for load in loads:
        load.start()

    barrier = pltpu.get_barrier_semaphore()
    for d in range(1, n):
        pl.semaphore_signal(
            barrier, inc=1, device_id={"expert": lax.rem(me + d, n)}, device_id_type=MESH
        )
    for where in (after, ahead):
        pl.semaphore_signal(barrier, inc=1, device_id={"section": where}, device_id_type=MESH)

    hit, _, f_pick, f_gate, f_place, f_back = route_tables(froute_ref[...], flogit_ref[...])
    _, b_select, b_pick, b_gate, b_place, b_back = route_tables(broute_ref[...], blogit_ref[...])
    place_out[0] = jnp.broadcast_to(f_place, place_out.shape[1:])
    place_out[1] = jnp.broadcast_to(b_place, place_out.shape[1:])
    logits = flogit_ref[...]
    raised = jnp.exp(logits - jnp.max(logits, axis=1, keepdims=True))
    probs = raised / jnp.sum(raised, axis=1, keepdims=True)
    both = jnp.concatenate(
        [jnp.sum(hit, axis=0, keepdims=True), jnp.sum(probs, axis=0, keepdims=True)], axis=0
    )
    row = iota((8, EXPERTS), 0)
    stats[me] = jnp.where(row == 0, both[0:1], jnp.where(row == 1, both[1:2], 0.0))

    pl.semaphore_wait(barrier, n + 1)

    def z_copy(which, src, dst, where):
        return pltpu.make_async_remote_copy(
            src_ref=src, dst_ref=dst, send_sem=z_send.at[which], recv_sem=z_recv.at[which],
            device_id={"section": where}, device_id_type=MESH,
        )

    places = [
        z_copy(0, place_out.at[0], place_in.at[0], ahead),
        z_copy(1, place_out.at[1], place_in.at[1], after),
    ]
    heads = [
        z_copy(2, head_out.at[0], head_in.at[0], after),
        z_copy(3, head_out.at[1], head_in.at[1], ahead),
    ]
    tails = [
        z_copy(4, tail_out.at[0], tail_in.at[0], after),
        z_copy(5, tail_out.at[1], tail_in.at[1], ahead),
    ]
    for copy in places:
        copy.start()

    def peer(d):
        return lax.rem(mine + d, half)

    def direct(kind, d):
        other = peer(d)
        return pltpu.make_async_remote_copy(
            src_ref=slab.at[kind, other // span], dst_ref=rx.at[kind, core, mine],
            send_sem=d_send.at[kind, other], recv_sem=d_recv.at[kind, mine],
            device_id={"expert": 2 * other + core}, device_id_type=MESH,
        )

    def arrival(kind, d):
        other = peer(d)
        return pltpu.make_async_remote_copy(
            src_ref=slab.at[kind, 0], dst_ref=rx.at[kind, core, other],
            send_sem=d_send.at[kind, other], recv_sem=d_recv.at[kind, other],
            device_id={"expert": 2 * other + core}, device_id_type=MESH,
        )

    def forward(kind, side, other):
        return pltpu.make_async_remote_copy(
            src_ref=rx.at[kind, side, other], dst_ref=rx.at[kind, side, other],
            send_sem=f_send.at[kind, other], recv_sem=f_recv.at[kind, other],
            device_id={"expert": sibling}, device_id_type=MESH,
        )

    def dispatch(kind):
        for d in range(1, half):
            direct(kind, d).start()
        rx[kind, core, mine] = slab[kind, mine // span]
        forward(kind, core, mine).start()

    def relay(kind):
        for d in range(1, half):
            arrival(kind, d).wait_recv()
            forward(kind, core, peer(d)).start()

    def complete(kind):
        for d in range(half):
            forward(kind, 1 - core, peer(d)).wait_recv()

    def to_slab(kind, rows, at):
        for e in range(EXP_WIN):
            slab[kind, e, :, at] = rows[e * CAP : (e + 1) * CAP].astype(BF16)

    def gather_saved(at, total):
        rows = dot(b_select, saved_ref[:, at])
        raw[:, at] = rows
        return total + jnp.sum(rows * rows, axis=1, keepdims=True)

    square = columns(width, gather_saved, jnp.zeros((SLOTS, 1), F32))
    saved_inv = lax.rsqrt(square / width + EPSILON)

    def norm_saved(at, carry):
        to_slab(0, raw[:, at] * saved_inv * gain_ref[:, at].astype(F32), at)
        return carry

    columns(width, norm_saved)
    dispatch(0)

    sources = (fwd_ref, bwd_ref)
    orders = []
    for which in range(2):
        places[which].wait_recv()
        orders.append(permutation(place_in[which, 0:1], tokens))

    for which in range(2):
        def fill_head(at, carry, which=which):
            head_out[which, :, at] = dot(orders[which][:HEAD], sources[which][:, at]).astype(BF16)
            return carry

        columns(width, fill_head)
        heads[which].start()
    for which in range(2):
        def fill_tail(at, carry, which=which):
            tail_out[which, :, at] = dot(orders[which][HEAD:], sources[which][:, at]).astype(BF16)
            return carry

        columns(width, fill_tail)
        tails[which].start()

    def stat(d):
        other = lax.rem(me + d, n)
        return pltpu.make_async_remote_copy(
            src_ref=stats.at[me], dst_ref=stats.at[me],
            send_sem=s_send.at[other], recv_sem=s_recv.at[me],
            device_id={"expert": other}, device_id_type=MESH,
        )

    def stat_arrival(d):
        other = lax.rem(me + d, n)
        return pltpu.make_async_remote_copy(
            src_ref=stats.at[other], dst_ref=stats.at[other],
            send_sem=s_send.at[other], recv_sem=s_recv.at[other],
            device_id={"expert": other}, device_id_type=MESH,
        )

    for d in range(1, n):
        stat(d).start()

    def arrived(kind, at):
        return rx[kind, :, :, :, at].astype(F32).reshape(n * CAP, CHUNK).astype(BF16)

    hidden = wg.shape[1]
    zero = jnp.zeros((n * CAP, hidden), F32)

    def gate_up(kind):
        def step(at, carry):
            rows = arrived(kind, at)
            return carry[0] + dot(rows, wg[at, :]), carry[1] + dot(rows, wu[at, :])

        return columns(width, step, (zero, zero))

    relay(0)
    loads[0].wait()
    loads[1].wait()
    complete(0)
    gate_b, up_b = gate_up(0)
    sigma = jax.nn.sigmoid(gate_b)
    terms[0] = up_b * sigma * (1.0 + gate_b * (1.0 - sigma))
    terms[1] = gate_b * sigma

    heads[1].wait_recv()

    def gather_grads(at, carry):
        to_slab(1, dot(b_pick, head_in[1, :, at]) * b_gate, at)
        return carry

    columns(width, gather_grads)
    dispatch(1)

    heads[0].wait_recv()

    def gather_fwd(at, total):
        rows = dot(f_pick, head_in[0, :, at])
        wide[:, at] = rows
        return total + jnp.sum(rows * rows, axis=1, keepdims=True)

    square = columns(width, gather_fwd, jnp.zeros((SLOTS, 1), F32))
    fwd_inv = lax.rsqrt(square / width + EPSILON)

    def norm_fwd(at, carry):
        to_slab(2, wide[:, at] * fwd_inv * gain_ref[:, at].astype(F32), at)
        return carry

    columns(width, norm_fwd)
    dispatch(2)
    relay(1)
    relay(2)
    loads[2].wait()
    complete(1)

    def pair(which):
        return pltpu.make_async_remote_copy(
            src_ref=part.at[which, 1 - core], dst_ref=pair_in.at[which],
            send_sem=p_send.at[which], recv_sem=p_recv.at[which],
            device_id={"expert": sibling}, device_id_type=MESH,
        )

    def to_home(which, d):
        other = peer(d)
        return pltpu.make_async_remote_copy(
            src_ref=summed.at[which, other], dst_ref=home.at[which, mine],
            send_sem=h_send.at[which, other], recv_sem=h_recv.at[which, mine],
            device_id={"expert": 2 * other + core}, device_id_type=MESH,
        )

    def from_holder(which, d):
        other = peer(d)
        return pltpu.make_async_remote_copy(
            src_ref=summed.at[which, other], dst_ref=home.at[which, other],
            send_sem=h_send.at[which, other], recv_sem=h_recv.at[which, other],
            device_id={"expert": 2 * other + core}, device_id_type=MESH,
        )

    def keep(which, rows, at):
        part[which, :, :, :, at] = rows.reshape(2, half, CAP, CHUNK).astype(BF16)

    def give(which):
        pair(which).wait_recv()

        def add(at, carry):
            total = part[which, core, :, :, at].astype(F32) + pair_in[which, :, :, at].astype(F32)
            summed[which, :, :, at] = total.astype(BF16)
            return carry

        columns(width, add)
        for d in range(1, half):
            to_home(which, d).start()
        home[which, mine] = summed[which, mine]

    d_hidden = columns(
        width,
        lambda at, total: total
        + lax.dot_general(arrived(1, at), wd[:, at], NT, preferred_element_type=F32),
        zero,
    )
    d_gate = (d_hidden * terms[0]).astype(BF16)
    d_up = (d_hidden * terms[1]).astype(BF16)

    def input_grad(at, carry):
        rows = lax.dot_general(d_gate, wg[at, :], NT, preferred_element_type=F32)
        rows = rows + lax.dot_general(d_up, wu[at, :], NT, preferred_element_type=F32)
        keep(0, rows, at)
        return carry

    columns(width, input_grad)
    pair(0).start()

    complete(2)
    gate_f, up_f = gate_up(2)
    hidden_rows = (gate_f * jax.nn.sigmoid(gate_f) * up_f).astype(BF16)
    give(0)

    def down(at, carry):
        keep(1, dot(hidden_rows, wd[:, at]), at)
        return carry

    columns(width, down)
    pair(1).start()

    for d in range(1, n):
        stat_arrival(d).wait_recv()
    counts = stats[0]
    for i in range(1, n):
        counts = counts + stats[i]
    tokens_all = tokens * n
    balance_ref[...] = (
        EXPERTS * (counts[0:1] / (tokens_all * TOPK)) * (counts[1:2] / tokens_all)
    )
    give(1)

    def returned(which, at):
        rows = []
        for e in range(EXP_WIN):
            total = home[which, e * span, :, at].astype(F32)
            for i in range(1, span):
                total = total + home[which, e * span + i, :, at].astype(F32)
            rows.append(total)
        return jnp.concatenate(rows, axis=0)

    def combine(back, which, rows, at):
        high, low = halves(rows)
        stack = jnp.concatenate([head_in[which, :, at], tail_in[which, :, at], high, low], axis=0)
        return dot(back, stack).astype(BF16)

    for d in range(1, half):
        from_holder(0, d).wait_recv()

    def weigh(at, total):
        weighted = returned(0, at) * gain_ref[:, at].astype(F32)
        wide[:, at] = weighted
        return total + jnp.sum(weighted * raw[:, at], axis=1, keepdims=True)

    mean = columns(width, weigh, jnp.zeros((SLOTS, 1), F32)) / width
    scale = saved_inv * saved_inv * saved_inv * mean
    tails[1].wait_recv()

    def finish_bwd(at, carry):
        rows = saved_inv * wide[:, at] - raw[:, at] * scale
        bout_ref[:, at] = combine(b_back, 1, rows, at)
        return carry

    columns(width, finish_bwd)

    for d in range(1, half):
        from_holder(1, d).wait_recv()
    tails[0].wait_recv()

    def finish_fwd(at, carry):
        fout_ref[:, at] = combine(f_back, 0, returned(1, at) * f_gate, at)
        return carry

    columns(width, finish_fwd)

    for copy in places + heads + tails:
        copy.wait_send()
    for kind in range(3):
        for d in range(half):
            forward(kind, core, peer(d)).wait_send()
        for d in range(1, half):
            direct(kind, d).wait_send()
    for which in range(2):
        pair(which).wait_send()
        for d in range(1, half):
            to_home(which, d).wait_send()
    for d in range(1, n):
        stat(d).wait_send()


def body(
    sections, n,
    fwd_sent, bwd_sent, bwd_saved, fwd_routes, bwd_routes, fwd_logits, bwd_logits,
    norm_gain, w_gate, w_up, w_down,
):
    tokens, width = fwd_sent.shape[1:]
    hidden = w_gate.shape[2]
    half = n // 2
    vmem = pl.BlockSpec(memory_space=pltpu.VMEM)
    hbm = pl.BlockSpec(memory_space=pl.ANY)
    dma = pltpu.SemaphoreType.DMA
    fwd_out, bwd_out, balance = pl.pallas_call(
        functools.partial(kernel, sections, n),
        out_shape=(
            jax.ShapeDtypeStruct((tokens, width), BF16),
            jax.ShapeDtypeStruct((tokens, width), BF16),
            jax.ShapeDtypeStruct((1, EXPERTS), F32),
        ),
        in_specs=[vmem] * 8 + [hbm] * 3,
        out_specs=(vmem, vmem, vmem),
        scratch_shapes=[
            pltpu.VMEM((width, hidden), BF16),
            pltpu.VMEM((width, hidden), BF16),
            pltpu.VMEM((hidden, width), BF16),
            pltpu.VMEM((2, 8, 2 * tokens), F32),
            pltpu.VMEM((2, 8, 2 * tokens), F32),
            pltpu.VMEM((2, HEAD, width), BF16),
            pltpu.VMEM((2, tokens - HEAD, width), BF16),
            pltpu.VMEM((2, HEAD, width), BF16),
            pltpu.VMEM((2, tokens - HEAD, width), BF16),
            pltpu.VMEM((3, EXP_WIN, CAP, width), BF16),
            pltpu.VMEM((3, 2, half, CAP, width), BF16),
            pltpu.VMEM((2, 2, half, CAP, width), BF16),
            pltpu.VMEM((2, half, CAP, width), BF16),
            pltpu.VMEM((2, half, CAP, width), BF16),
            pltpu.VMEM((2, half, CAP, width), BF16),
            pltpu.VMEM((SLOTS, width), F32),
            pltpu.VMEM((SLOTS, width), F32),
            pltpu.VMEM((2, n * CAP, hidden), F32),
            pltpu.VMEM((n, 8, EXPERTS), F32),
            dma((3,)), dma((6,)), dma((6,)),
            dma((3, half)), dma((3, half)), dma((3, half)), dma((3, half)),
            dma((2,)), dma((2,)), dma((2, half)), dma((2, half)),
            dma((n,)), dma((n,)),
        ],
        compiler_params=pltpu.CompilerParams(
            collective_id=0, has_side_effects=True, vmem_limit_bytes=52 * 1024 * 1024
        ),
    )(
        fwd_sent[0], bwd_sent[0], bwd_saved[0], fwd_routes[0], bwd_routes[0],
        fwd_logits[0], bwd_logits[0], norm_gain, w_gate[0], w_up[0], w_down[0],
    )
    return fwd_out[None], bwd_out[None], balance


def solution(mesh):
    block = P("section", "expert", None)
    return jax.shard_map(
        functools.partial(body, mesh.shape["section"], mesh.shape["expert"]),
        mesh=mesh,
        in_specs=(block,) * 7
        + (
            P("section", None),
            P("section", None, "expert"),
            P("section", None, "expert"),
            P("section", "expert", None),
        ),
        out_specs=(block, block, P("section", None)),
        check_vma=False,
    )
```

time: 107 us -> 57.5 us (0.54); the launches traced: 105 us -> 57 us
  Pallas kernels: 0 us -> 49.5 us
  matrix products: 30.9 us -> 0 us
  starting transfers between devices: 25.9 us -> 0 us
  waiting for transfers between devices: 15.3 us -> 0 us
  blocking collectives: 15.1 us -> 0 us
  other arithmetic: 12.5 us -> 0 us
  local copies, waits for them, and re-layouts: 4.78 us -> 6.91 us
    pallas_call x0 -> x1, Pallas kernels: none -> 49.5 us  [body(): pl.pallas_call(functools.partial(kernel, sections, n), out_shape=(jax.Sha...]
    dot_general x11 -> x0, matrix products: 30.9 us -> none  [the longest x1 4.9 us: expert_backward(): lax.dot_general(d_gate, gate_slab, contract, preferred_element_type=jnp.f...]
    all_to_all x5 -> x0, starting transfers between devices: 20.7 us -> none  [the longest x1 4.15 us: body(): lax.all_to_all(expert_backward(lax.all_to_all(saved_send, 'expert', split...]
    all_to_all x5 -> x0, waiting for transfers between devices: 15.3 us -> none  [the longest x1 7.13 us: body(): lax.all_to_all(grad_send, 'expert', split_axis=0, concat_axis=0, tiled=True)]
    psum x1 -> x0, blocking collectives: 15.1 us -> none  [body(): counts, prob_sums = lax.psum((counts, prob_sums), 'expert')]
    unnamed x12 -> x13, local copies, waits for them, and re-layouts: 0.88 us -> 6.91 us
    reduce_sum x14 -> x0, other arithmetic: 5.81 us -> none  [the longest x2 2.49 us: norm_rows(): jnp.mean(widened * widened, axis=-1, keepdims=True) + epsilon]
    ppermute x2 -> x0, starting transfers between devices: 5.16 us -> none  [from_behind(): return lax.ppermute(block, axis, route)]
  transfers between devices with their start and end apart: 7 -> 0, of which waited for: 3 -> 0; matrix products, arithmetic and copies ran while one was open for 39% -> 0% of each run, Pallas kernels for 0% -> 0%
where the time goes in v1:
time: 57.5 us; the launch traced here: 57 us
  Pallas kernels  49.5 us (86%)
  local copies, waits for them, and re-layouts  6.91 us (12%)
  between operations  0.64 us (1%)
    pallas_call x1, Pallas kernels, body(): pl.pallas_call(functools.partial(kernel, sections, n), out_shape=(jax.Sha...  49.5 us
    unnamed x13, local copies, waits for them, and re-layouts  6.91 us

profile of v1, /device:TPU:0, one launch (start us, length us, event | category | flops | bytes accessed | tf_op | source)
XLA Modules:
  0.0 57.0 jit_solution(763219987552300603)
XLA Ops:
  0.6 0.8 %copy.14 = s32[1,64,8]{2,1,0:T(8,128)S(1)} copy(s32[1,64,8]{1,2,0:T(8,128)} %param.14) | data formatting | bytes 4096 | tf_op args[3]
  1.4 0.8 %copy.15 = s32[1,64,8]{2,1,0:T(8,128)S(1)} copy(s32[1,64,8]{1,2,0:T(8,128)} %param.15) | data formatting | bytes 4096 | tf_op args[4]
  2.2 0.0 copy-start
  2.2 1.0 %copy-done = bf16[1,64,4096]{2,1,0:T(8,128)(2,1)S(1)} copy-done((bf16[1,64,4096]{2,1,0:T(8,128)(2,1)S(1)}, bf16[1,64,4096]{2,1,0:T(8,128)(2,1)}, u32[]{:S(2)}) %copy-start) | copy-done | bytes 524312
  3.2 0.0 copy-start.1
  3.2 0.8 %copy-done.1 = f32[1,64,128]{2,1,0:T(8,128)S(1)} copy-done((f32[1,64,128]{2,1,0:T(8,128)S(1)}, f32[1,64,128]{2,1,0:T(8,128)}, u32[]{:S(2)}) %copy-start.1) | copy-done | bytes 32792
  4.0 0.0 copy-start.2
  4.0 0.8 %copy-done.2 = f32[1,64,128]{2,1,0:T(8,128)S(1)} copy-done((f32[1,64,128]{2,1,0:T(8,128)S(1)}, f32[1,64,128]{2,1,0:T(8,128)}, u32[]{:S(2)}) %copy-start.2) | copy-done | bytes 32792
  4.7 0.0 copy-start.3
  4.7 0.7 %copy-done.3 = bf16[1,4096]{1,0:T(2,128)(2,1)S(1)} copy-done((bf16[1,4096]{1,0:T(2,128)(2,1)S(1)}, bf16[1,4096]{1,0:T(2,128)(2,1)}, u32[]{:S(2)}) %copy-start.3) | copy-done | bytes 8216
  5.4 49.5 %shard_map.130 = (bf16[64,4096]{1,0:T(8,128)(2,1)S(1)}, bf16[64,4096]{1,0:T(8,128)(2,1)S(1)}, f32[1,128]{1,0:T(1,128)S(1)}) custom-call(bf16[64,4096]{1,0:T(8,128)(2,1)S(1)} %bitcast.12, bf16[64,4096]{1,0:T(8,128)(2,1)} %bitcast.22, bf16[64,4096]{1,0:T(8,128)(2,1)} %bitcast.23, s32[64,8]{1,0:T(8,128)S(1)} %bitcast.15, s32[64,8]{1,0:T(8,128)S(1)} %bitcast.16, ...), custom_call_target="tpu_custom_call" | custom-call | tf_op jit(solution)/shard_map/pallas_call | solution.py:470
  54.9 0.8 %copy.19 = bf16[1,64,4096]{2,1,0:T(8,128)(2,1)} copy(bf16[1,64,4096]{2,1,0:T(8,128)(2,1)S(1)} %bitcast.14) | data formatting | bytes 1048576
  55.7 0.8 %copy.20 = bf16[1,64,4096]{2,1,0:T(8,128)(2,1)} copy(bf16[1,64,4096]{2,1,0:T(8,128)(2,1)S(1)} %bitcast.13) | data formatting | bytes 1048576
  56.5 0.5 copy.21
Async XLA Ops:
  2.2 1.0 %copy-start = (bf16[1,64,4096]{2,1,0:T(8,128)(2,1)S(1)}, bf16[1,64,4096]{2,1,0:T(8,128)(2,1)}, u32[]{:S(2)}) copy-start(bf16[1,64,4096]{2,1,0:T(8,128)(2,1)} %param.11) | copy-start | bytes 1572868
  3.2 0.8 %copy-start.1 = (f32[1,64,128]{2,1,0:T(8,128)S(1)}, f32[1,64,128]{2,1,0:T(8,128)}, u32[]{:S(2)}) copy-start(f32[1,64,128]{2,1,0:T(8,128)} %param.16) | copy-start | bytes 98308
  4.0 0.8 %copy-start.2 = (f32[1,64,128]{2,1,0:T(8,128)S(1)}, f32[1,64,128]{2,1,0:T(8,128)}, u32[]{:S(2)}) copy-start(f32[1,64,128]{2,1,0:T(8,128)} %param.17) | copy-start | bytes 98308
  4.7 0.7 %copy-start.3 = (bf16[1,4096]{1,0:T(2,128)(2,1)S(1)}, bf16[1,4096]{1,0:T(2,128)(2,1)}, u32[]{:S(2)}) copy-start(bf16[1,4096]{1,0:T(2,128)(2,1)} %gain_ref.1) | copy-start | bytes 24580

commit v2 on v1

--- a/solution.py
+++ b/solution.py
@@ -14,6 +14,7 @@
 SLOTS = EXP_WIN * CAP
 HEAD = 16
 CHUNK = 512
+PIECES = 2
 EPSILON = 1e-06
 MESH = pl.DeviceIdType.MESH
 F32 = jnp.float32
@@ -39,9 +40,13 @@
 def route_tables(routes, logits):
     tokens, experts = logits.shape
     lane = iota((tokens, experts), 1)
-    chosen = routes[:, 0:1] == lane
+    unit = (iota((tokens, tokens), 0) == iota((tokens, tokens), 1)).astype(BF16)
+    routes = lax.dot_general(
+        unit, routes.astype(F32).astype(BF16), NT, preferred_element_type=F32
+    )
+    chosen = routes[:, 0:1] == lane.astype(F32)
     for k in range(1, TOPK):
-        chosen = chosen | (routes[:, k : k + 1] == lane)
+        chosen = chosen | (routes[:, k : k + 1] == lane.astype(F32))
     hit = chosen.astype(F32)
     top = jnp.max(jnp.where(chosen, logits, -jnp.inf), axis=1, keepdims=True)
     raised = jnp.exp(jnp.where(chosen, logits, top) - top) * hit
@@ -71,12 +76,10 @@
     taken, gated = slot_at(lane)
     taken = jnp.where(lane < SLOTS, taken, 0.0)
     gated = jnp.where(lane < SLOTS, gated, 0.0)
-    taken = jnp.where(lane == SLOTS, place, taken)
     turned = jnp.concatenate([taken, gated], axis=0).T
     select = turned[:SLOTS, :tokens].astype(BF16)
     right = iota((SLOTS, 2 * tokens), 1) >= tokens
     gate_slot = jnp.sum(jnp.where(right, turned[:SLOTS], 0.0), axis=1, keepdims=True)
-    place_row = turned[SLOTS : SLOTS + 1]
     again = lane - tokens
     again = jnp.where(again >= SLOTS, again - SLOTS, again)
     back = jnp.where(
@@ -85,11 +88,22 @@
         jnp.where(lane < tokens + 2 * SLOTS, slot_at(again)[0], 0.0),
     ).astype(BF16)
     head_select = dot(select, back[:, :HEAD]).astype(BF16)
-    return hit, select, head_select, gate_slot, place_row, back[:, : tokens + 2 * SLOTS]
-
-
-def permutation(place_row, tokens):
-    return (iota((tokens, tokens), 0).astype(F32) == place_row[:, :tokens]).astype(BF16)
+    return hit, select, head_select, gate_slot, back[:, : tokens + 2 * SLOTS]
+
+
+def place_row(routes):
+    tokens = routes.shape[1]
+    here = jnp.max(jnp.where(routes < EXP_WIN, 1.0, 0.0), axis=0, keepdims=True)
+    here = jnp.broadcast_to(here, (8, tokens))
+    above = (iota((tokens, tokens), 0) < iota((tokens, tokens), 1)).astype(BF16)
+    before = dot(here.astype(BF16), above)
+    count = jnp.sum(here, axis=1, keepdims=True)
+    order = iota((8, tokens), 1).astype(F32)
+    return jnp.where(here > 0.0, before, count + order - before)
+
+
+def permutation(place, tokens):
+    return (iota((tokens, tokens), 0).astype(F32) == place).astype(BF16)
 
 
 def halves(rows):
@@ -99,9 +113,10 @@
 
 def kernel(
     sections, n,
-    fwd_ref, bwd_ref, saved_ref, froute_ref, broute_ref, flogit_ref, blogit_ref, gain_ref,
+    froute_hbm, broute_hbm, flogit_hbm, blogit_hbm, fwd_hbm, bwd_hbm, saved_hbm, gain_hbm,
     wg_hbm, wu_hbm, wd_hbm,
     fout_ref, bout_ref, balance_ref,
+    froute_ref, broute_ref, flogit_ref, blogit_ref, fwd_ref, bwd_ref, saved_ref, gain_ref,
     wg, wu, wd, place_out, place_in, head_out, tail_out, head_in, tail_in,
     slab, rx, part, pair_in, summed, home, raw, wide, terms, stats,
     w_sem, z_send, z_recv, d_send, d_recv, f_send, f_recv,
@@ -117,7 +132,12 @@
 
     loads = [
         pltpu.make_async_copy(src, dst, w_sem.at[i])
-        for i, (src, dst) in enumerate(((wg_hbm, wg), (wu_hbm, wu), (wd_hbm, wd)))
+        for i, (src, dst) in enumerate((
+            (froute_hbm, froute_ref), (broute_hbm, broute_ref),
+            (flogit_hbm, flogit_ref), (blogit_hbm, blogit_ref),
+            (fwd_hbm, fwd_ref), (bwd_hbm, bwd_ref), (saved_hbm, saved_ref), (gain_hbm, gain_ref),
+            (wg_hbm, wg), (wu_hbm, wu), (wd_hbm, wd),
+        ))
     ]
     for load in loads:
         load.start()
@@ -130,19 +150,10 @@
     for where in (after, ahead):
         pl.semaphore_signal(barrier, inc=1, device_id={"section": where}, device_id_type=MESH)
 
-    hit, _, f_pick, f_gate, f_place, f_back = route_tables(froute_ref[...], flogit_ref[...])
-    _, b_select, b_pick, b_gate, b_place, b_back = route_tables(broute_ref[...], blogit_ref[...])
-    place_out[0] = jnp.broadcast_to(f_place, place_out.shape[1:])
-    place_out[1] = jnp.broadcast_to(b_place, place_out.shape[1:])
-    logits = flogit_ref[...]
-    raised = jnp.exp(logits - jnp.max(logits, axis=1, keepdims=True))
-    probs = raised / jnp.sum(raised, axis=1, keepdims=True)
-    both = jnp.concatenate(
-        [jnp.sum(hit, axis=0, keepdims=True), jnp.sum(probs, axis=0, keepdims=True)], axis=0
-    )
-    row = iota((8, EXPERTS), 0)
-    stats[me] = jnp.where(row == 0, both[0:1], jnp.where(row == 1, both[1:2], 0.0))
-
+    loads[0].wait()
+    loads[1].wait()
+    place_out[0] = place_row(froute_ref[...])
+    place_out[1] = place_row(broute_ref[...])
     pl.semaphore_wait(barrier, n + 1)
 
     def z_copy(which, src, dst, where):
@@ -166,6 +177,11 @@
     for copy in places:
         copy.start()
 
+    loads[2].wait()
+    loads[3].wait()
+    hit, _, f_pick, f_gate, f_back = route_tables(froute_ref[...], flogit_ref[...])
+    _, b_select, b_pick, b_gate, b_back = route_tables(broute_ref[...], blogit_ref[...])
+
     def peer(d):
         return lax.rem(mine + d, half)
 
@@ -211,21 +227,8 @@
         for e in range(EXP_WIN):
             slab[kind, e, :, at] = rows[e * CAP : (e + 1) * CAP].astype(BF16)
 
-    def gather_saved(at, total):
-        rows = dot(b_select, saved_ref[:, at])
-        raw[:, at] = rows
-        return total + jnp.sum(rows * rows, axis=1, keepdims=True)
-
-    square = columns(width, gather_saved, jnp.zeros((SLOTS, 1), F32))
-    saved_inv = lax.rsqrt(square / width + EPSILON)
-
-    def norm_saved(at, carry):
-        to_slab(0, raw[:, at] * saved_inv * gain_ref[:, at].astype(F32), at)
-        return carry
-
-    columns(width, norm_saved)
-    dispatch(0)
-
+    loads[4].wait()
+    loads[5].wait()
     sources = (fwd_ref, bwd_ref)
     orders = []
     for which in range(2):
@@ -239,13 +242,39 @@
 
         columns(width, fill_head)
         heads[which].start()
+
+    loads[6].wait()
+    loads[7].wait()
+
+    def gather_saved(at, total):
+        rows = dot(b_select, saved_ref[:, at])
+        raw[:, at] = rows
+        return total + jnp.sum(rows * rows, axis=1, keepdims=True)
+
+    square = columns(width, gather_saved, jnp.zeros((SLOTS, 1), F32))
+    saved_inv = lax.rsqrt(square / width + EPSILON)
+
+    def norm_saved(at, carry):
+        to_slab(0, raw[:, at] * saved_inv * gain_ref[:, at].astype(F32), at)
+        return carry
+
+    columns(width, norm_saved)
+    dispatch(0)
+
     for which in range(2):
         def fill_tail(at, carry, which=which):
             tail_out[which, :, at] = dot(orders[which][HEAD:], sources[which][:, at]).astype(BF16)
             return carry
 
         columns(width, fill_tail)
-        tails[which].start()
+
+    logits = flogit_ref[...]
+    raised = jnp.exp(logits - jnp.max(logits, axis=1, keepdims=True))
+    probs = raised / jnp.sum(raised, axis=1, keepdims=True)
+    count_row = jnp.sum(hit, axis=0, keepdims=True)
+    prob_row = jnp.sum(probs, axis=0, keepdims=True)
+    row = iota((8, EXPERTS), 0)
+    stats[me] = jnp.where(row == 0, count_row, jnp.where(row == 1, prob_row, 0.0))
 
     def stat(d):
         other = lax.rem(me + d, n)
@@ -280,82 +309,97 @@
         return columns(width, step, (zero, zero))
 
     relay(0)
-    loads[0].wait()
-    loads[1].wait()
+
+    heads[1].wait_recv()
+
+    def gather_grads(at, carry):
+        to_slab(1, dot(b_pick, head_in[1, :, at]) * b_gate, at)
+        return carry
+
+    columns(width, gather_grads)
+    dispatch(1)
+
+    heads[0].wait_recv()
+
+    def gather_fwd(at, total):
+        rows = dot(f_pick, head_in[0, :, at])
+        wide[:, at] = rows
+        return total + jnp.sum(rows * rows, axis=1, keepdims=True)
+
+    square = columns(width, gather_fwd, jnp.zeros((SLOTS, 1), F32))
+    fwd_inv = lax.rsqrt(square / width + EPSILON)
+
+    def norm_fwd(at, carry):
+        to_slab(2, wide[:, at] * fwd_inv * gain_ref[:, at].astype(F32), at)
+        return carry
+
+    columns(width, norm_fwd)
+    dispatch(2)
+    for copy in tails:
+        copy.start()
+
+    loads[8].wait()
+    loads[9].wait()
     complete(0)
     gate_b, up_b = gate_up(0)
     sigma = jax.nn.sigmoid(gate_b)
     terms[0] = up_b * sigma * (1.0 + gate_b * (1.0 - sigma))
     terms[1] = gate_b * sigma
-
-    heads[1].wait_recv()
-
-    def gather_grads(at, carry):
-        to_slab(1, dot(b_pick, head_in[1, :, at]) * b_gate, at)
-        return carry
-
-    columns(width, gather_grads)
-    dispatch(1)
-
-    heads[0].wait_recv()
-
-    def gather_fwd(at, total):
-        rows = dot(f_pick, head_in[0, :, at])
-        wide[:, at] = rows
-        return total + jnp.sum(rows * rows, axis=1, keepdims=True)
-
-    square = columns(width, gather_fwd, jnp.zeros((SLOTS, 1), F32))
-    fwd_inv = lax.rsqrt(square / width + EPSILON)
-
-    def norm_fwd(at, carry):
-        to_slab(2, wide[:, at] * fwd_inv * gain_ref[:, at].astype(F32), at)
-        return carry
-
-    columns(width, norm_fwd)
-    dispatch(2)
     relay(1)
     relay(2)
-    loads[2].wait()
+    loads[10].wait()
     complete(1)
 
-    def pair(which):
-        return pltpu.make_async_remote_copy(
-            src_ref=part.at[which, 1 - core], dst_ref=pair_in.at[which],
-            send_sem=p_send.at[which], recv_sem=p_recv.at[which],
+    piece = width // PIECES
+
+    def pair(which, p):
+        return pltpu.make_async_remote_copy(
+            src_ref=part.at[which, p, 1 - core], dst_ref=pair_in.at[which, p],
+            send_sem=p_send.at[which, p], recv_sem=p_recv.at[which, p],
             device_id={"expert": sibling}, device_id_type=MESH,
         )
 
-    def to_home(which, d):
+    def to_home(which, p, d):
         other = peer(d)
         return pltpu.make_async_remote_copy(
-            src_ref=summed.at[which, other], dst_ref=home.at[which, mine],
-            send_sem=h_send.at[which, other], recv_sem=h_recv.at[which, mine],
+            src_ref=summed.at[which, p, other], dst_ref=home.at[which, p, mine],
+            send_sem=h_send.at[which, p, other], recv_sem=h_recv.at[which, p, mine],
             device_id={"expert": 2 * other + core}, device_id_type=MESH,
         )
 
-    def from_holder(which, d):
+    def from_holder(which, p, d):
         other = peer(d)
         return pltpu.make_async_remote_copy(
-            src_ref=summed.at[which, other], dst_ref=home.at[which, other],
-            send_sem=h_send.at[which, other], recv_sem=h_recv.at[which, other],
+            src_ref=summed.at[which, p, other], dst_ref=home.at[which, p, other],
+            send_sem=h_send.at[which, p, other], recv_sem=h_recv.at[which, p, other],
             device_id={"expert": 2 * other + core}, device_id_type=MESH,
         )
 
-    def keep(which, rows, at):
-        part[which, :, :, :, at] = rows.reshape(2, half, CAP, CHUNK).astype(BF16)
-
-    def give(which):
-        pair(which).wait_recv()
+    def pieces(which, make):
+        for p in range(PIECES):
+            def fill(i, carry, p=p):
+                at = pl.ds(pl.multiple_of(i * CHUNK, CHUNK), CHUNK)
+                full = pl.ds(pl.multiple_of(p * piece + i * CHUNK, CHUNK), CHUNK)
+                rows = make(full)
+                part[which, p, :, :, :, at] = rows.reshape(2, half, CAP, CHUNK).astype(BF16)
+                return carry
+
+            lax.fori_loop(0, piece // CHUNK, fill, 0)
+            pair(which, p).start()
+
+    def give(which, p):
+        pair(which, p).wait_recv()
 
         def add(at, carry):
-            total = part[which, core, :, :, at].astype(F32) + pair_in[which, :, :, at].astype(F32)
-            summed[which, :, :, at] = total.astype(BF16)
+            total = part[which, p, core, :, :, at].astype(F32)
+            total = total + pair_in[which, p, :, :, at].astype(F32)
+            summed[which, p, :, :, at] = total.astype(BF16)
             return carry
 
-        columns(width, add)
+        columns(piece, add)
         for d in range(1, half):
-            to_home(which, d).start()
-        home[which, mine] = summed[which, mine]
+            to_home(which, p, d).start()
+        home[which, p, mine] = summed[which, p, mine]
 
     d_hidden = columns(
         width,
@@ -366,26 +410,19 @@
     d_gate = (d_hidden * terms[0]).astype(BF16)
     d_up = (d_hidden * terms[1]).astype(BF16)
 
-    def input_grad(at, carry):
+    def input_grad(at):
         rows = lax.dot_general(d_gate, wg[at, :], NT, preferred_element_type=F32)
-        rows = rows + lax.dot_general(d_up, wu[at, :], NT, preferred_element_type=F32)
-        keep(0, rows, at)
-        return carry
-
-    columns(width, input_grad)
-    pair(0).start()
-
+        return rows + lax.dot_general(d_up, wu[at, :], NT, preferred_element_type=F32)
+
+    pieces(0, input_grad)
     complete(2)
+    for p in range(PIECES):
+        give(0, p)
     gate_f, up_f = gate_up(2)
     hidden_rows = (gate_f * jax.nn.sigmoid(gate_f) * up_f).astype(BF16)
-    give(0)
-
-    def down(at, carry):
-        keep(1, dot(hidden_rows, wd[:, at]), at)
-        return carry
-
-    columns(width, down)
-    pair(1).start()
+    pieces(1, lambda at: dot(hidden_rows, wd[:, at]))
+    for p in range(PIECES):
+        give(1, p)
 
     for d in range(1, n):
         stat_arrival(d).wait_recv()
@@ -396,32 +433,41 @@
     balance_ref[...] = (
         EXPERTS * (counts[0:1] / (tokens_all * TOPK)) * (counts[1:2] / tokens_all)
     )
-    give(1)
-
-    def returned(which, at):
+
+    def returned(which, p, at):
         rows = []
         for e in range(EXP_WIN):
-            total = home[which, e * span, :, at].astype(F32)
+            total = home[which, p, e * span, :, at].astype(F32)
             for i in range(1, span):
-                total = total + home[which, e * span + i, :, at].astype(F32)
+                total = total + home[which, p, e * span + i, :, at].astype(F32)
             rows.append(total)
         return jnp.concatenate(rows, axis=0)
+
+    def by_piece(which, p, step, init):
+        for d in range(1, half):
+            from_holder(which, p, d).wait_recv()
+
+        def run(i, carry):
+            at = pl.ds(pl.multiple_of(i * CHUNK, CHUNK), CHUNK)
+            full = pl.ds(pl.multiple_of(p * piece + i * CHUNK, CHUNK), CHUNK)
+            return step(full, returned(which, p, at), carry)
+
+        return lax.fori_loop(0, piece // CHUNK, run, init)
 
     def combine(back, which, rows, at):
         high, low = halves(rows)
         stack = jnp.concatenate([head_in[which, :, at], tail_in[which, :, at], high, low], axis=0)
         return dot(back, stack).astype(BF16)
 
-    for d in range(1, half):
-        from_holder(0, d).wait_recv()
-
-    def weigh(at, total):
-        weighted = returned(0, at) * gain_ref[:, at].astype(F32)
+    def weigh(at, rows, total):
+        weighted = rows * gain_ref[:, at].astype(F32)
         wide[:, at] = weighted
         return total + jnp.sum(weighted * raw[:, at], axis=1, keepdims=True)
 
-    mean = columns(width, weigh, jnp.zeros((SLOTS, 1), F32)) / width
-    scale = saved_inv * saved_inv * saved_inv * mean
+    total = jnp.zeros((SLOTS, 1), F32)
+    for p in range(PIECES):
+        total = by_piece(0, p, weigh, total)
+    scale = saved_inv * saved_inv * saved_inv * (total / width)
     tails[1].wait_recv()
 
     def finish_bwd(at, carry):
@@ -430,16 +476,14 @@
         return carry
 
     columns(width, finish_bwd)
-
-    for d in range(1, half):
-        from_holder(1, d).wait_recv()
     tails[0].wait_recv()
 
-    def finish_fwd(at, carry):
-        fout_ref[:, at] = combine(f_back, 0, returned(1, at) * f_gate, at)
+    def finish_fwd(at, rows, carry):
+        fout_ref[:, at] = combine(f_back, 0, rows * f_gate, at)
         return carry
 
-    columns(width, finish_fwd)
+    for p in range(PIECES):
+        by_piece(1, p, finish_fwd, 0)
 
     for copy in places + heads + tails:
         copy.wait_send()
@@ -449,9 +493,10 @@
         for d in range(1, half):
             direct(kind, d).wait_send()
     for which in range(2):
-        pair(which).wait_send()
-        for d in range(1, half):
-            to_home(which, d).wait_send()
+        for p in range(PIECES):
+            pair(which, p).wait_send()
+            for d in range(1, half):
+                to_home(which, p, d).wait_send()
     for d in range(1, n):
         stat(d).wait_send()
 
@@ -474,39 +519,47 @@
             jax.ShapeDtypeStruct((tokens, width), BF16),
             jax.ShapeDtypeStruct((1, EXPERTS), F32),
         ),
-        in_specs=[vmem] * 8 + [hbm] * 3,
+        in_specs=[hbm] * 11,
         out_specs=(vmem, vmem, vmem),
         scratch_shapes=[
+            pltpu.VMEM((TOPK, tokens), jnp.int32),
+            pltpu.VMEM((TOPK, tokens), jnp.int32),
+            pltpu.VMEM((tokens, EXPERTS), F32),
+            pltpu.VMEM((tokens, EXPERTS), F32),
+            pltpu.VMEM((tokens, width), BF16),
+            pltpu.VMEM((tokens, width), BF16),
+            pltpu.VMEM((tokens, width), BF16),
+            pltpu.VMEM((1, width), BF16),
             pltpu.VMEM((width, hidden), BF16),
             pltpu.VMEM((width, hidden), BF16),
             pltpu.VMEM((hidden, width), BF16),
-            pltpu.VMEM((2, 8, 2 * tokens), F32),
-            pltpu.VMEM((2, 8, 2 * tokens), F32),
+            pltpu.VMEM((2, 8, tokens), F32),
+            pltpu.VMEM((2, 8, tokens), F32),
             pltpu.VMEM((2, HEAD, width), BF16),
             pltpu.VMEM((2, tokens - HEAD, width), BF16),
             pltpu.VMEM((2, HEAD, width), BF16),
             pltpu.VMEM((2, tokens - HEAD, width), BF16),
             pltpu.VMEM((3, EXP_WIN, CAP, width), BF16),
             pltpu.VMEM((3, 2, half, CAP, width), BF16),
-            pltpu.VMEM((2, 2, half, CAP, width), BF16),
-            pltpu.VMEM((2, half, CAP, width), BF16),
-            pltpu.VMEM((2, half, CAP, width), BF16),
-            pltpu.VMEM((2, half, CAP, width), BF16),
+            pltpu.VMEM((2, PIECES, 2, half, CAP, width // PIECES), BF16),
+            pltpu.VMEM((2, PIECES, half, CAP, width // PIECES), BF16),
+            pltpu.VMEM((2, PIECES, half, CAP, width // PIECES), BF16),
+            pltpu.VMEM((2, PIECES, half, CAP, width // PIECES), BF16),
             pltpu.VMEM((SLOTS, width), F32),
             pltpu.VMEM((SLOTS, width), F32),
             pltpu.VMEM((2, n * CAP, hidden), F32),
             pltpu.VMEM((n, 8, EXPERTS), F32),
-            dma((3,)), dma((6,)), dma((6,)),
+            dma((11,)), dma((6,)), dma((6,)),
             dma((3, half)), dma((3, half)), dma((3, half)), dma((3, half)),
-            dma((2,)), dma((2,)), dma((2, half)), dma((2, half)),
+            dma((2, PIECES)), dma((2, PIECES)), dma((2, PIECES, half)), dma((2, PIECES, half)),
             dma((n,)), dma((n,)),
         ],
         compiler_params=pltpu.CompilerParams(
-            collective_id=0, has_side_effects=True, vmem_limit_bytes=52 * 1024 * 1024
+            collective_id=0, has_side_effects=True, vmem_limit_bytes=60 * 1024 * 1024
         ),
     )(
-        fwd_sent[0], bwd_sent[0], bwd_saved[0], fwd_routes[0], bwd_routes[0],
-        fwd_logits[0], bwd_logits[0], norm_gain, w_gate[0], w_up[0], w_down[0],
+        fwd_routes[0].T, bwd_routes[0].T, fwd_logits[0], bwd_logits[0],
+        fwd_sent[0], bwd_sent[0], bwd_saved[0], norm_gain, w_gate[0], w_up[0], w_down[0],
     )
     return fwd_out[None], bwd_out[None], balance
 

time: 57.5 us -> 48.7 us (0.85)
  Pallas kernels: 49.5 us -> 43 us
  local copies, waits for them, and re-layouts: 6.91 us -> 4.85 us
    pallas_call x1, Pallas kernels: 49.5 us -> 43 us  [body(): pl.pallas_call(functools.partial(kernel, sections, n), out_shape=(jax.Sha...]
    unnamed x13 -> x3, local copies, waits for them, and re-layouts: 6.91 us -> 4.85 us
where the time goes in v2:
time: 48.7 us; the launch traced here: 48.4 us
  Pallas kernels  43 us (88%)
  local copies, waits for them, and re-layouts  4.85 us (10%)
  between operations  0.64 us (1%)
    pallas_call x1, Pallas kernels, body(): pl.pallas_call(functools.partial(kernel, sections, n), out_shape=(jax.Sha...  43 us
    unnamed x3, local copies, waits for them, and re-layouts  4.85 us

profile of v2, /device:TPU:0, one launch (start us, length us, event | category | flops | bytes accessed | tf_op | source)
XLA Modules:
  0.0 48.4 jit_solution(4781625977038102335)
XLA Ops:
  0.6 43.0 %shard_map.130 = (bf16[64,4096]{1,0:T(8,128)(2,1)}, bf16[64,4096]{1,0:T(8,128)(2,1)}, f32[1,128]{1,0:T(1,128)}) custom-call(s32[8,64]{1,0:T(8,128)} %bitcast.26, s32[8,64]{1,0:T(8,128)} %bitcast.27, f32[64,128]{1,0:T(8,128)} %bitcast.24, f32[64,128]{1,0:T(8,128)} %bitcast.25, bf16[64,4096]{1,0:T(8,128)(2,1)} %bitcast.19, bf16[64,4096]{1,0:T(8,128)(2,1)} %bitcast.20, ...), custom_call_target="tpu_custom_call" | custom-call | tf_op jit(solution)/shard_map/pallas_call | solution.py:515
  43.6 1.9 %copy.17 = bf16[1,64,4096]{2,1,0:T(8,128)(2,1)} copy(bf16[1,64,4096]{2,1,0:T(8,128)(2,1)} %bitcast.23) | data formatting | bytes 1048576
  45.5 1.9 %copy.18 = bf16[1,64,4096]{2,1,0:T(8,128)(2,1)} copy(bf16[1,64,4096]{2,1,0:T(8,128)(2,1)} %bitcast.22) | data formatting | bytes 1048576
  47.3 1.1 %copy.19 = f32[1,128]{1,0:T(1,128)} copy(f32[1,128]{1,0:T(1,128)} %get-tuple-element.14) | data formatting | bytes 1024

commit v3 on v2

--- a/solution.py
+++ b/solution.py
@@ -13,7 +13,8 @@
 CAP = 8
 SLOTS = EXP_WIN * CAP
 HEAD = 16
-CHUNK = 512
+CHUNK = 1024
+WIDE = 2048
 PIECES = 2
 EPSILON = 1e-06
 MESH = pl.DeviceIdType.MESH
@@ -30,11 +31,14 @@
     return jnp.dot(a, b, preferred_element_type=F32)
 
 
-def columns(width, body, init=0):
+def columns(width, body, init=0, chunk=1024):
+    if chunk >= width:
+        return body(pl.ds(0, width), init)
+
     def step(i, carry):
-        return body(pl.ds(pl.multiple_of(i * CHUNK, CHUNK), CHUNK), carry)
-
-    return lax.fori_loop(0, width // CHUNK, step, init)
+        return body(pl.ds(pl.multiple_of(i * chunk, chunk), chunk), carry)
+
+    return lax.fori_loop(0, width // chunk, step, init)
 
 
 def route_tables(routes, logits):
@@ -88,7 +92,7 @@
         jnp.where(lane < tokens + 2 * SLOTS, slot_at(again)[0], 0.0),
     ).astype(BF16)
     head_select = dot(select, back[:, :HEAD]).astype(BF16)
-    return hit, select, head_select, gate_slot, back[:, : tokens + 2 * SLOTS]
+    return hit, select, head_select, gate_slot, back
 
 
 def place_row(routes):
@@ -108,21 +112,24 @@
 
 def halves(rows):
     high = rows.astype(BF16)
-    return high, (rows - high.astype(F32)).astype(BF16)
+    low = (rows - high.astype(F32)).astype(BF16)
+    return jnp.concatenate([high, low], axis=0)
 
 
 def kernel(
     sections, n,
     froute_hbm, broute_hbm, flogit_hbm, blogit_hbm, fwd_hbm, bwd_hbm, saved_hbm, gain_hbm,
     wg_hbm, wu_hbm, wd_hbm,
-    fout_ref, bout_ref, balance_ref,
+    stack_hbm, back_hbm, balance_hbm,
     froute_ref, broute_ref, flogit_ref, blogit_ref, fwd_ref, bwd_ref, saved_ref, gain_ref,
-    wg, wu, wd, place_out, place_in, head_out, tail_out, head_in, tail_in,
+    wgu, wd, place_out, place_in, head_out, tail_out, head_in,
+    halved, back_ref, balance_ref,
     slab, rx, part, pair_in, summed, home, raw, wide, terms, stats,
-    w_sem, z_send, z_recv, d_send, d_recv, f_send, f_recv,
+    w_sem, o_sem, z_send, z_recv, d_send, d_recv, f_send, f_recv,
     p_send, p_recv, h_send, h_recv, s_send, s_recv,
 ):
     tokens, width = fwd_ref.shape
+    hidden = wd.shape[0]
     half = n // 2
     span = half // EXP_WIN
     sec, me = lax.axis_index("section"), lax.axis_index("expert")
@@ -130,13 +137,18 @@
     sibling = me + 1 - 2 * core
     after, ahead = lax.rem(sec + 1, sections), lax.rem(sec + sections - 1, sections)
 
+    joined = wgu.shape[0] == 1
+    if joined:
+        gate_side, up_side = (wgu.at[0, :, pl.ds(i * hidden, hidden)] for i in range(2))
+    else:
+        gate_side, up_side = wgu.at[0], wgu.at[1]
     loads = [
         pltpu.make_async_copy(src, dst, w_sem.at[i])
         for i, (src, dst) in enumerate((
             (froute_hbm, froute_ref), (broute_hbm, broute_ref),
             (flogit_hbm, flogit_ref), (blogit_hbm, blogit_ref),
             (fwd_hbm, fwd_ref), (bwd_hbm, bwd_ref), (saved_hbm, saved_ref), (gain_hbm, gain_ref),
-            (wg_hbm, wg), (wu_hbm, wu), (wd_hbm, wd),
+            (wg_hbm, gate_side), (wu_hbm, up_side), (wd_hbm, wd),
         ))
     ]
     for load in loads:
@@ -171,8 +183,12 @@
         z_copy(3, head_out.at[1], head_in.at[1], ahead),
     ]
     tails = [
-        z_copy(4, tail_out.at[0], tail_in.at[0], after),
-        z_copy(5, tail_out.at[1], tail_in.at[1], ahead),
+        z_copy(4, tail_out.at[0], stack_hbm.at[0, pl.ds(HEAD, tokens - HEAD)], after),
+        z_copy(5, tail_out.at[1], stack_hbm.at[1, pl.ds(HEAD, tokens - HEAD)], ahead),
+    ]
+    head_keep = [
+        pltpu.make_async_copy(head_in.at[i], stack_hbm.at[i, pl.ds(0, HEAD)], o_sem.at[i])
+        for i in range(2)
     ]
     for copy in places:
         copy.start()
@@ -181,6 +197,11 @@
     loads[3].wait()
     hit, _, f_pick, f_gate, f_back = route_tables(froute_ref[...], flogit_ref[...])
     _, b_select, b_pick, b_gate, b_back = route_tables(broute_ref[...], blogit_ref[...])
+
+    back_ref[0] = f_back
+    back_ref[1] = b_back
+    back_keep = pltpu.make_async_copy(back_ref, back_hbm, o_sem.at[2])
+    back_keep.start()
 
     def peer(d):
         return lax.rem(mine + d, half)
@@ -240,7 +261,7 @@
             head_out[which, :, at] = dot(orders[which][:HEAD], sources[which][:, at]).astype(BF16)
             return carry
 
-        columns(width, fill_head)
+        columns(width, fill_head, chunk=WIDE)
         heads[which].start()
 
     loads[6].wait()
@@ -251,14 +272,14 @@
         raw[:, at] = rows
         return total + jnp.sum(rows * rows, axis=1, keepdims=True)
 
-    square = columns(width, gather_saved, jnp.zeros((SLOTS, 1), F32))
+    square = columns(width, gather_saved, jnp.zeros((SLOTS, 1), F32), chunk=WIDE)
     saved_inv = lax.rsqrt(square / width + EPSILON)
 
     def norm_saved(at, carry):
         to_slab(0, raw[:, at] * saved_inv * gain_ref[:, at].astype(F32), at)
         return carry
 
-    columns(width, norm_saved)
+    columns(width, norm_saved, chunk=WIDE)
     dispatch(0)
 
     for which in range(2):
@@ -298,45 +319,49 @@
     def arrived(kind, at):
         return rx[kind, :, :, :, at].astype(F32).reshape(n * CAP, CHUNK).astype(BF16)
 
-    hidden = wg.shape[1]
     zero = jnp.zeros((n * CAP, hidden), F32)
 
     def gate_up(kind):
-        def step(at, carry):
+        def step(at, totals):
             rows = arrived(kind, at)
-            return carry[0] + dot(rows, wg[at, :]), carry[1] + dot(rows, wu[at, :])
-
-        return columns(width, step, (zero, zero))
+            return tuple(total + dot(rows, wgu[i, at, :]) for i, total in enumerate(totals))
+
+        empty = jnp.zeros((n * CAP, wgu.shape[2]), F32)
+        totals = columns(width, step, (empty,) * wgu.shape[0])
+        return (totals[0][:, :hidden], totals[0][:, hidden:]) if joined else totals
 
     relay(0)
 
     heads[1].wait_recv()
+    heads[0].wait_recv()
+    for copy in tails:
+        copy.start()
+    for copy in head_keep:
+        copy.start()
+
 
     def gather_grads(at, carry):
         to_slab(1, dot(b_pick, head_in[1, :, at]) * b_gate, at)
         return carry
 
-    columns(width, gather_grads)
+    columns(width, gather_grads, chunk=WIDE)
     dispatch(1)
 
-    heads[0].wait_recv()
 
     def gather_fwd(at, total):
         rows = dot(f_pick, head_in[0, :, at])
         wide[:, at] = rows
         return total + jnp.sum(rows * rows, axis=1, keepdims=True)
 
-    square = columns(width, gather_fwd, jnp.zeros((SLOTS, 1), F32))
+    square = columns(width, gather_fwd, jnp.zeros((SLOTS, 1), F32), chunk=WIDE)
     fwd_inv = lax.rsqrt(square / width + EPSILON)
 
     def norm_fwd(at, carry):
         to_slab(2, wide[:, at] * fwd_inv * gain_ref[:, at].astype(F32), at)
         return carry
 
-    columns(width, norm_fwd)
+    columns(width, norm_fwd, chunk=WIDE)
     dispatch(2)
-    for copy in tails:
-        copy.start()
 
     loads[8].wait()
     loads[9].wait()
@@ -407,19 +432,23 @@
         + lax.dot_general(arrived(1, at), wd[:, at], NT, preferred_element_type=F32),
         zero,
     )
-    d_gate = (d_hidden * terms[0]).astype(BF16)
-    d_up = (d_hidden * terms[1]).astype(BF16)
+    d_parts = [(d_hidden * terms[i]).astype(BF16) for i in range(2)]
+    if joined:
+        d_parts = [jnp.concatenate(d_parts, axis=1)]
 
     def input_grad(at):
-        rows = lax.dot_general(d_gate, wg[at, :], NT, preferred_element_type=F32)
-        return rows + lax.dot_general(d_up, wu[at, :], NT, preferred_element_type=F32)
+        return sum(
+            lax.dot_general(d_part, wgu[i, at, :], NT, preferred_element_type=F32)
+            for i, d_part in enumerate(d_parts)
+        )
 
     pieces(0, input_grad)
     complete(2)
-    for p in range(PIECES):
-        give(0, p)
+    give(0, 0)
     gate_f, up_f = gate_up(2)
     hidden_rows = (gate_f * jax.nn.sigmoid(gate_f) * up_f).astype(BF16)
+    for p in range(1, PIECES):
+        give(0, p)
     pieces(1, lambda at: dot(hidden_rows, wd[:, at]))
     for p in range(PIECES):
         give(1, p)
@@ -433,6 +462,8 @@
     balance_ref[...] = (
         EXPERTS * (counts[0:1] / (tokens_all * TOPK)) * (counts[1:2] / tokens_all)
     )
+    balance_keep = pltpu.make_async_copy(balance_ref, balance_hbm, o_sem.at[3])
+    balance_keep.start()
 
     def returned(which, p, at):
         rows = []
@@ -454,11 +485,6 @@
 
         return lax.fori_loop(0, piece // CHUNK, run, init)
 
-    def combine(back, which, rows, at):
-        high, low = halves(rows)
-        stack = jnp.concatenate([head_in[which, :, at], tail_in[which, :, at], high, low], axis=0)
-        return dot(back, stack).astype(BF16)
-
     def weigh(at, rows, total):
         weighted = rows * gain_ref[:, at].astype(F32)
         wide[:, at] = weighted
@@ -468,23 +494,35 @@
     for p in range(PIECES):
         total = by_piece(0, p, weigh, total)
     scale = saved_inv * saved_inv * saved_inv * (total / width)
-    tails[1].wait_recv()
+
+    def rows_copy(which, at, i):
+        rows = pl.ds(tokens, 2 * SLOTS)
+        return pltpu.make_async_copy(
+            halved.at[which, :, at], stack_hbm.at[which, rows, at], o_sem.at[4 + i]
+        )
 
     def finish_bwd(at, carry):
         rows = saved_inv * wide[:, at] - raw[:, at] * scale
-        bout_ref[:, at] = combine(b_back, 1, rows, at)
+        halved[1, :, at] = halves(rows)
         return carry
 
-    columns(width, finish_bwd)
-    tails[0].wait_recv()
+    columns(width, finish_bwd, chunk=WIDE)
+    kept = [rows_copy(1, pl.ds(0, width), PIECES)]
+    kept[0].start()
 
     def finish_fwd(at, rows, carry):
-        fout_ref[:, at] = combine(f_back, 0, rows * f_gate, at)
+        halved[0, :, at] = halves(rows * f_gate)
         return carry
 
     for p in range(PIECES):
         by_piece(1, p, finish_fwd, 0)
-
+        kept.append(rows_copy(0, pl.ds(p * piece, piece), p))
+        kept[-1].start()
+
+    for copy in tails:
+        copy.wait_recv()
+    for copy in head_keep + [back_keep, balance_keep] + kept:
+        copy.wait()
     for copy in places + heads + tails:
         copy.wait_send()
     for kind in range(3):
@@ -501,6 +539,41 @@
         stat(d).wait_send()
 
 
+def place_kernel(
+    stack_hbm, back_hbm, balance_hbm, fout_hbm, bout_hbm, out_hbm,
+    stack, back, balance, out, in_sem, out_sem, small_sem,
+):
+    _, rows, width = stack.shape
+    steps = width // CHUNK
+    spans = [pl.ds(i * CHUNK, CHUNK) for i in range(steps)]
+    small = [
+        pltpu.make_async_copy(back_hbm, back, small_sem.at[0]),
+        pltpu.make_async_copy(balance_hbm, balance, small_sem.at[1]),
+    ]
+    loads = [
+        pltpu.make_async_copy(stack_hbm.at[:, :, at], stack.at[:, :, at], in_sem.at[i])
+        for i, at in enumerate(spans)
+    ]
+    for copy in small + loads:
+        copy.start()
+    small[1].wait()
+    last = pltpu.make_async_copy(balance, out_hbm, small_sem.at[2])
+    last.start()
+    small[0].wait()
+    stores = []
+    for i, at in enumerate(spans):
+        loads[i].wait()
+        for which, target in enumerate((fout_hbm, bout_hbm)):
+            out[which, :, at] = dot(back[which, :, :rows], stack[which, :, at]).astype(BF16)
+            store = pltpu.make_async_copy(
+                out.at[which, :, at], target.at[:, at], out_sem.at[which, i]
+            )
+            store.start()
+            stores.append(store)
+    for copy in stores + [last]:
+        copy.wait()
+
+
 def body(
     sections, n,
     fwd_sent, bwd_sent, bwd_saved, fwd_routes, bwd_routes, fwd_logits, bwd_logits,
@@ -509,18 +582,18 @@
     tokens, width = fwd_sent.shape[1:]
     hidden = w_gate.shape[2]
     half = n // 2
-    vmem = pl.BlockSpec(memory_space=pltpu.VMEM)
     hbm = pl.BlockSpec(memory_space=pl.ANY)
     dma = pltpu.SemaphoreType.DMA
-    fwd_out, bwd_out, balance = pl.pallas_call(
+    rows = tokens + 2 * SLOTS
+    stack, back, balance = pl.pallas_call(
         functools.partial(kernel, sections, n),
         out_shape=(
-            jax.ShapeDtypeStruct((tokens, width), BF16),
-            jax.ShapeDtypeStruct((tokens, width), BF16),
+            jax.ShapeDtypeStruct((2, rows, width), BF16),
+            jax.ShapeDtypeStruct((2, tokens, EXPERTS), BF16),
             jax.ShapeDtypeStruct((1, EXPERTS), F32),
         ),
         in_specs=[hbm] * 11,
-        out_specs=(vmem, vmem, vmem),
+        out_specs=(hbm, hbm, hbm),
         scratch_shapes=[
             pltpu.VMEM((TOPK, tokens), jnp.int32),
             pltpu.VMEM((TOPK, tokens), jnp.int32),
@@ -530,15 +603,16 @@
             pltpu.VMEM((tokens, width), BF16),
             pltpu.VMEM((tokens, width), BF16),
             pltpu.VMEM((1, width), BF16),
-            pltpu.VMEM((width, hidden), BF16),
-            pltpu.VMEM((width, hidden), BF16),
+            pltpu.VMEM((1, width, 2 * hidden) if hidden % 128 == 0 else (2, width, hidden), BF16),
             pltpu.VMEM((hidden, width), BF16),
             pltpu.VMEM((2, 8, tokens), F32),
             pltpu.VMEM((2, 8, tokens), F32),
             pltpu.VMEM((2, HEAD, width), BF16),
             pltpu.VMEM((2, tokens - HEAD, width), BF16),
             pltpu.VMEM((2, HEAD, width), BF16),
-            pltpu.VMEM((2, tokens - HEAD, width), BF16),
+            pltpu.VMEM((2, 2 * SLOTS, width), BF16),
+            pltpu.VMEM((2, tokens, EXPERTS), BF16),
+            pltpu.VMEM((1, EXPERTS), F32),
             pltpu.VMEM((3, EXP_WIN, CAP, width), BF16),
             pltpu.VMEM((3, 2, half, CAP, width), BF16),
             pltpu.VMEM((2, PIECES, 2, half, CAP, width // PIECES), BF16),
@@ -549,7 +623,7 @@
             pltpu.VMEM((SLOTS, width), F32),
             pltpu.VMEM((2, n * CAP, hidden), F32),
             pltpu.VMEM((n, 8, EXPERTS), F32),
-            dma((11,)), dma((6,)), dma((6,)),
+            dma((11,)), dma((5 + PIECES,)), dma((6,)), dma((6,)),
             dma((3, half)), dma((3, half)), dma((3, half)), dma((3, half)),
             dma((2, PIECES)), dma((2, PIECES)), dma((2, PIECES, half)), dma((2, PIECES, half)),
             dma((n,)), dma((n,)),
@@ -561,6 +635,24 @@
         fwd_routes[0].T, bwd_routes[0].T, fwd_logits[0], bwd_logits[0],
         fwd_sent[0], bwd_sent[0], bwd_saved[0], norm_gain, w_gate[0], w_up[0], w_down[0],
     )
+    fwd_out, bwd_out, balance = pl.pallas_call(
+        place_kernel,
+        out_shape=(
+            jax.ShapeDtypeStruct((tokens, width), BF16),
+            jax.ShapeDtypeStruct((tokens, width), BF16),
+            jax.ShapeDtypeStruct((1, EXPERTS), F32),
+        ),
+        in_specs=[hbm] * 3,
+        out_specs=(hbm, hbm, hbm),
+        scratch_shapes=[
+            pltpu.VMEM((2, rows, width), BF16),
+            pltpu.VMEM((2, tokens, EXPERTS), BF16),
+            pltpu.VMEM((1, EXPERTS), F32),
+            pltpu.VMEM((2, tokens, width), BF16),
+            dma((width // CHUNK,)), dma((2, width // CHUNK)), dma((3,)),
+        ],
+        compiler_params=pltpu.CompilerParams(vmem_limit_bytes=60 * 1024 * 1024),
+    )(stack, back, balance)
     return fwd_out[None], bwd_out[None], balance
 
 

time: 48.7 us -> 39.6 us (0.81)
  local copies, waits for them, and re-layouts: 4.85 us -> 0 us
  Pallas kernels: 43 us -> 38.8 us
    pallas_call x1, Pallas kernels: 43 us -> 36.1 us  [body(): pl.pallas_call(functools.partial(kernel, sections, n), out_shape=(jax.Sha...]
    unnamed x3 -> x0, local copies, waits for them, and re-layouts: 4.85 us -> none
    pallas_call x0 -> x1, Pallas kernels: none -> 2.65 us  [body(): pl.pallas_call(place_kernel, out_shape=(jax.ShapeDtypeStruct((tokens, wid...]
where the time goes in v3:
time: 39.6 us; the launch traced here: 39.4 us
  Pallas kernels  38.8 us (98%)
  between operations  0.64 us (2%)
    pallas_call x1, Pallas kernels, body(): pl.pallas_call(functools.partial(kernel, sections, n), out_shape=(jax.Sha...  36.1 us
    pallas_call x1, Pallas kernels, body(): pl.pallas_call(place_kernel, out_shape=(jax.ShapeDtypeStruct((tokens, wid...  2.65 us

profile of v3, /device:TPU:0, one launch (start us, length us, event | category | flops | bytes accessed | tf_op | source)
XLA Modules:
  0.0 39.4 jit_solution(5035236556389558054)
XLA Ops:
  0.6 36.1 %shard_map.130 = (bf16[2,96,4096]{2,1,0:T(8,128)(2,1)}, bf16[2,64,128]{2,1,0:T(8,128)(2,1)}, f32[1,128]{1,0:T(1,128)}) custom-call(s32[8,64]{1,0:T(8,128)} %bitcast.24, s32[8,64]{1,0:T(8,128)} %bitcast.25, f32[64,128]{1,0:T(8,128)} %bitcast.22, f32[64,128]{1,0:T(8,128)} %bitcast.23, bf16[64,4096]{1,0:T(8,128)(2,1)} %bitcast.19, bf16[64,4096]{1,0:T(8,128)(2,1)} %bitcast.20, ...), custom_call_target="tpu_custom_call" | custom-call | tf_op jit(solution)/shard_map/pallas_call | solution.py:588
  36.8 2.6 %shard_map.131 = (bf16[64,4096]{1,0:T(8,128)(2,1)}, bf16[64,4096]{1,0:T(8,128)(2,1)}, f32[1,128]{1,0:T(1,128)}) custom-call(bf16[2,96,4096]{2,1,0:T(8,128)(2,1)} %get-tuple-element.9.stack_hbm, bf16[2,64,128]{2,1,0:T(8,128)(2,1)} %get-tuple-element.10.back_hbm, f32[1,128]{1,0:T(1,128)} %get-tuple-element.11.balance_hbm), custom_call_target="tpu_custom_call" | custom-call | tf_op jit(solution)/shard_map/pallas_call | solution.py:638

commit v4 on v3

--- a/solution.py
+++ b/solution.py
@@ -15,7 +15,7 @@
 HEAD = 16
 CHUNK = 1024
 WIDE = 2048
-PIECES = 2
+PIECES = 4
 EPSILON = 1e-06
 MESH = pl.DeviceIdType.MESH
 F32 = jnp.float32
@@ -371,7 +371,6 @@
     terms[0] = up_b * sigma * (1.0 + gate_b * (1.0 - sigma))
     terms[1] = gate_b * sigma
     relay(1)
-    relay(2)
     loads[10].wait()
     complete(1)
 
@@ -400,17 +399,10 @@
             device_id={"expert": 2 * other + core}, device_id_type=MESH,
         )
 
-    def pieces(which, make):
-        for p in range(PIECES):
-            def fill(i, carry, p=p):
-                at = pl.ds(pl.multiple_of(i * CHUNK, CHUNK), CHUNK)
-                full = pl.ds(pl.multiple_of(p * piece + i * CHUNK, CHUNK), CHUNK)
-                rows = make(full)
-                part[which, p, :, :, :, at] = rows.reshape(2, half, CAP, CHUNK).astype(BF16)
-                return carry
-
-            lax.fori_loop(0, piece // CHUNK, fill, 0)
-            pair(which, p).start()
+    def make_piece(which, p, make):
+        rows = make(pl.ds(p * piece, piece))
+        part[which, p] = rows.reshape(2, half, CAP, piece).astype(BF16)
+        pair(which, p).start()
 
     def give(which, p):
         pair(which, p).wait_recv()
@@ -442,16 +434,26 @@
             for i, d_part in enumerate(d_parts)
         )
 
-    pieces(0, input_grad)
+    make_piece(0, 0, input_grad)
+    make_piece(0, 1, input_grad)
+    give(0, 0)
+    relay(2)
+    for p in range(2, PIECES):
+        make_piece(0, p, input_grad)
+        give(0, p - 1)
     complete(2)
-    give(0, 0)
     gate_f, up_f = gate_up(2)
     hidden_rows = (gate_f * jax.nn.sigmoid(gate_f) * up_f).astype(BF16)
+    give(0, PIECES - 1)
+
+    def down(at):
+        return dot(hidden_rows, wd[:, at])
+
+    make_piece(1, 0, down)
     for p in range(1, PIECES):
-        give(0, p)
-    pieces(1, lambda at: dot(hidden_rows, wd[:, at]))
-    for p in range(PIECES):
-        give(1, p)
+        make_piece(1, p, down)
+        give(1, p - 1)
+    give(1, PIECES - 1)
 
     for d in range(1, n):
         stat_arrival(d).wait_recv()
@@ -478,12 +480,8 @@
         for d in range(1, half):
             from_holder(which, p, d).wait_recv()
 
-        def run(i, carry):
-            at = pl.ds(pl.multiple_of(i * CHUNK, CHUNK), CHUNK)
-            full = pl.ds(pl.multiple_of(p * piece + i * CHUNK, CHUNK), CHUNK)
-            return step(full, returned(which, p, at), carry)
-
-        return lax.fori_loop(0, piece // CHUNK, run, init)
+        at = pl.ds(0, piece)
+        return step(pl.ds(p * piece, piece), returned(which, p, at), init)
 
     def weigh(at, rows, total):
         weighted = rows * gain_ref[:, at].astype(F32)

time: 39.6 us -> 40 us (1.010)
  no operation moved by 1% of the time
where the time goes in v4:
time: 40 us; the launch traced here: 39.8 us
  Pallas kernels  39.1 us (98%)
  between operations  0.64 us (2%)
    pallas_call x1, Pallas kernels, body(): pl.pallas_call(functools.partial(kernel, sections, n), out_shape=(jax.Sha...  36.5 us
    pallas_call x1, Pallas kernels, body(): pl.pallas_call(place_kernel, out_shape=(jax.ShapeDtypeStruct((tokens, wid...  2.65 us

profile of v4, /device:TPU:0, one launch (start us, length us, event | category | flops | bytes accessed | tf_op | source)
XLA Modules:
  0.0 39.8 jit_solution(18082304144876261197)
XLA Ops:
  0.6 36.5 %shard_map.130 = (bf16[2,96,4096]{2,1,0:T(8,128)(2,1)}, bf16[2,64,128]{2,1,0:T(8,128)(2,1)}, f32[1,128]{1,0:T(1,128)}) custom-call(s32[8,64]{1,0:T(8,128)} %bitcast.24, s32[8,64]{1,0:T(8,128)} %bitcast.25, f32[64,128]{1,0:T(8,128)} %bitcast.22, f32[64,128]{1,0:T(8,128)} %bitcast.23, bf16[64,4096]{1,0:T(8,128)(2,1)} %bitcast.19, bf16[64,4096]{1,0:T(8,128)(2,1)} %bitcast.20, ...), custom_call_target="tpu_custom_call" | custom-call | tf_op jit(solution)/shard_map/pallas_call | solution.py:586
  37.1 2.6 %shard_map.131 = (bf16[64,4096]{1,0:T(8,128)(2,1)}, bf16[64,4096]{1,0:T(8,128)(2,1)}, f32[1,128]{1,0:T(1,128)}) custom-call(bf16[2,96,4096]{2,1,0:T(8,128)(2,1)} %get-tuple-element.9.stack_hbm, bf16[2,64,128]{2,1,0:T(8,128)(2,1)} %get-tuple-element.10.back_hbm, f32[1,128]{1,0:T(1,128)} %get-tuple-element.11.balance_hbm), custom_call_target="tpu_custom_call" | custom-call | tf_op jit(solution)/shard_map/pallas_call | solution.py:636

commit v5 on v4

--- a/solution.py
+++ b/solution.py
@@ -15,6 +15,8 @@
 HEAD = 16
 CHUNK = 1024
 WIDE = 2048
+RAW = 1024
+REST = 1536
 PIECES = 4
 EPSILON = 1e-06
 MESH = pl.DeviceIdType.MESH
@@ -39,6 +41,17 @@
         return body(pl.ds(pl.multiple_of(i * chunk, chunk), chunk), carry)
 
     return lax.fori_loop(0, width // chunk, step, init)
+
+
+def after_raw(width, body, init=0, chunk=CHUNK):
+    def step(i, carry):
+        return body(
+            pl.ds(pl.multiple_of(i * chunk, chunk), chunk),
+            pl.ds(pl.multiple_of(RAW + i * chunk, 512), chunk),
+            carry,
+        )
+
+    return lax.fori_loop(0, (width - RAW) // chunk, step, init)
 
 
 def route_tables(routes, logits):
@@ -86,13 +99,13 @@
     gate_slot = jnp.sum(jnp.where(right, turned[:SLOTS], 0.0), axis=1, keepdims=True)
     again = lane - tokens
     again = jnp.where(again >= SLOTS, again - SLOTS, again)
-    back = jnp.where(
-        lane < tokens,
-        (place == lane.astype(F32)).astype(F32),
-        jnp.where(lane < tokens + 2 * SLOTS, slot_at(again)[0], 0.0),
-    ).astype(BF16)
+    slots_back = jnp.where(lane < tokens + 2 * SLOTS, slot_at(again)[0], 0.0)
+    back, plain = (
+        jnp.where(lane < tokens, (at == lane).astype(F32), slots_back).astype(BF16)
+        for at in (place.astype(jnp.int32), iota((tokens, experts), 0))
+    )
     head_select = dot(select, back[:, :HEAD]).astype(BF16)
-    return hit, select, head_select, gate_slot, back
+    return hit, select, head_select, gate_slot, back, plain
 
 
 def place_row(routes):
@@ -123,7 +136,7 @@
     stack_hbm, back_hbm, balance_hbm,
     froute_ref, broute_ref, flogit_ref, blogit_ref, fwd_ref, bwd_ref, saved_ref, gain_ref,
     wgu, wd, place_out, place_in, head_out, tail_out, head_in,
-    halved, back_ref, balance_ref,
+    raw_in, halved, back_ref, balance_ref,
     slab, rx, part, pair_in, summed, home, raw, wide, terms, stats,
     w_sem, o_sem, z_send, z_recv, d_send, d_recv, f_send, f_recv,
     p_send, p_recv, h_send, h_recv, s_send, s_recv,
@@ -151,7 +164,7 @@
             (wg_hbm, gate_side), (wu_hbm, up_side), (wd_hbm, wd),
         ))
     ]
-    for load in loads:
+    for load in loads[:8]:
         load.start()
 
     barrier = pltpu.get_barrier_semaphore()
@@ -173,6 +186,11 @@
             src_ref=src, dst_ref=dst, send_sem=z_send.at[which], recv_sem=z_recv.at[which],
             device_id={"section": where}, device_id_type=MESH,
         )
+
+    past = pl.ds(RAW, width - RAW)
+
+    def tail_place(which):
+        return stack_hbm.at[which, pl.ds(HEAD, tokens - HEAD), past]
 
     places = [
         z_copy(0, place_out.at[0], place_in.at[0], ahead),
@@ -183,25 +201,30 @@
         z_copy(3, head_out.at[1], head_in.at[1], ahead),
     ]
     tails = [
-        z_copy(4, tail_out.at[0], stack_hbm.at[0, pl.ds(HEAD, tokens - HEAD)], after),
-        z_copy(5, tail_out.at[1], stack_hbm.at[1, pl.ds(HEAD, tokens - HEAD)], ahead),
+        z_copy(4, tail_out.at[0], tail_place(0), after),
+        z_copy(5, tail_out.at[1], tail_place(1), ahead),
+    ]
+    raws = [
+        z_copy(6, fwd_ref.at[:, pl.ds(0, RAW)], raw_in.at[0], after),
+        z_copy(7, bwd_ref.at[:, pl.ds(0, RAW)], raw_in.at[1], ahead),
     ]
     head_keep = [
-        pltpu.make_async_copy(head_in.at[i], stack_hbm.at[i, pl.ds(0, HEAD)], o_sem.at[i])
+        pltpu.make_async_copy(head_in.at[i], stack_hbm.at[i, pl.ds(0, HEAD), past], o_sem.at[i])
+        for i in range(2)
+    ] + [
+        pltpu.make_async_copy(
+            raw_in.at[i], stack_hbm.at[i, pl.ds(0, tokens), pl.ds(0, RAW)],
+            o_sem.at[5 + PIECES + i],
+        )
         for i in range(2)
     ]
     for copy in places:
         copy.start()
-
-    loads[2].wait()
-    loads[3].wait()
-    hit, _, f_pick, f_gate, f_back = route_tables(froute_ref[...], flogit_ref[...])
-    _, b_select, b_pick, b_gate, b_back = route_tables(broute_ref[...], blogit_ref[...])
-
-    back_ref[0] = f_back
-    back_ref[1] = b_back
-    back_keep = pltpu.make_async_copy(back_ref, back_hbm, o_sem.at[2])
-    back_keep.start()
+    for which in range(2):
+        loads[4 + which].wait()
+        raws[which].start()
+    for load in loads[8:]:
+        load.start()
 
     def peer(d):
         return lax.rem(mine + d, half)
@@ -248,8 +271,8 @@
         for e in range(EXP_WIN):
             slab[kind, e, :, at] = rows[e * CAP : (e + 1) * CAP].astype(BF16)
 
-    loads[4].wait()
-    loads[5].wait()
+    loads[3].wait()
+    _, b_select, b_pick, b_gate, b_back, b_plain = route_tables(broute_ref[...], blogit_ref[...])
     sources = (fwd_ref, bwd_ref)
     orders = []
     for which in range(2):
@@ -257,12 +280,22 @@
         orders.append(permutation(place_in[which, 0:1], tokens))
 
     for which in range(2):
-        def fill_head(at, carry, which=which):
-            head_out[which, :, at] = dot(orders[which][:HEAD], sources[which][:, at]).astype(BF16)
+        def fill_head(at, full, carry, which=which):
+            rows = dot(orders[which][:HEAD], sources[which][:, full])
+            head_out[which, :, at] = rows.astype(BF16)
             return carry
 
-        columns(width, fill_head, chunk=WIDE)
+        after_raw(width, fill_head, chunk=REST)
         heads[which].start()
+
+    loads[2].wait()
+    hit, f_select, f_pick, f_gate, f_back, f_plain = route_tables(
+        froute_ref[...], flogit_ref[...]
+    )
+    for i, table in enumerate((f_back, f_plain, b_back, b_plain)):
+        back_ref[i] = table
+    back_keep = pltpu.make_async_copy(back_ref, back_hbm, o_sem.at[2])
+    back_keep.start()
 
     loads[6].wait()
     loads[7].wait()
@@ -283,11 +316,12 @@
     dispatch(0)
 
     for which in range(2):
-        def fill_tail(at, carry, which=which):
-            tail_out[which, :, at] = dot(orders[which][HEAD:], sources[which][:, at]).astype(BF16)
+        def fill_tail(at, full, carry, which=which):
+            rows = dot(orders[which][HEAD:], sources[which][:, full])
+            tail_out[which, :, at] = rows.astype(BF16)
             return carry
 
-        columns(width, fill_tail)
+        after_raw(width, fill_tail)
 
     logits = flogit_ref[...]
     raised = jnp.exp(logits - jnp.max(logits, axis=1, keepdims=True))
@@ -332,28 +366,33 @@
 
     relay(0)
 
-    heads[1].wait_recv()
-    heads[0].wait_recv()
-    for copy in tails:
-        copy.start()
+    for which in range(2):
+        heads[which].wait_send()
+        tails[which].start()
+    for copy in raws + heads:
+        copy.wait_recv()
     for copy in head_keep:
         copy.start()
 
 
-    def gather_grads(at, carry):
-        to_slab(1, dot(b_pick, head_in[1, :, at]) * b_gate, at)
+    def gather_grads(at, full, carry):
+        to_slab(1, dot(b_pick, head_in[1, :, at]) * b_gate, full)
         return carry
 
-    columns(width, gather_grads, chunk=WIDE)
+    to_slab(1, dot(b_select, raw_in[1]) * b_gate, pl.ds(0, RAW))
+    after_raw(width, gather_grads, chunk=REST)
     dispatch(1)
 
 
-    def gather_fwd(at, total):
+    def gather_fwd(at, full, total):
         rows = dot(f_pick, head_in[0, :, at])
-        wide[:, at] = rows
+        wide[:, full] = rows
         return total + jnp.sum(rows * rows, axis=1, keepdims=True)
 
-    square = columns(width, gather_fwd, jnp.zeros((SLOTS, 1), F32), chunk=WIDE)
+    first = dot(f_select, raw_in[0])
+    wide[:, pl.ds(0, RAW)] = first
+    square = jnp.sum(first * first, axis=1, keepdims=True)
+    square = after_raw(width, gather_fwd, square, chunk=REST)
     fwd_inv = lax.rsqrt(square / width + EPSILON)
 
     def norm_fwd(at, carry):
@@ -521,7 +560,7 @@
         copy.wait_recv()
     for copy in head_keep + [back_keep, balance_keep] + kept:
         copy.wait()
-    for copy in places + heads + tails:
+    for copy in places + raws + tails:
         copy.wait_send()
     for kind in range(3):
         for d in range(half):
@@ -542,8 +581,8 @@
     stack, back, balance, out, in_sem, out_sem, small_sem,
 ):
     _, rows, width = stack.shape
-    steps = width // CHUNK
-    spans = [pl.ds(i * CHUNK, CHUNK) for i in range(steps)]
+    steps = width // RAW
+    spans = [pl.ds(i * RAW, RAW) for i in range(steps)]
     small = [
         pltpu.make_async_copy(back_hbm, back, small_sem.at[0]),
         pltpu.make_async_copy(balance_hbm, balance, small_sem.at[1]),
@@ -562,7 +601,8 @@
     for i, at in enumerate(spans):
         loads[i].wait()
         for which, target in enumerate((fout_hbm, bout_hbm)):
-            out[which, :, at] = dot(back[which, :, :rows], stack[which, :, at]).astype(BF16)
+            table = back[2 * which + (1 if i == 0 else 0), :, :rows]
+            out[which, :, at] = dot(table, stack[which, :, at]).astype(BF16)
             store = pltpu.make_async_copy(
                 out.at[which, :, at], target.at[:, at], out_sem.at[which, i]
             )
@@ -587,7 +627,7 @@
         functools.partial(kernel, sections, n),
         out_shape=(
             jax.ShapeDtypeStruct((2, rows, width), BF16),
-            jax.ShapeDtypeStruct((2, tokens, EXPERTS), BF16),
+            jax.ShapeDtypeStruct((4, tokens, EXPERTS), BF16),
             jax.ShapeDtypeStruct((1, EXPERTS), F32),
         ),
         in_specs=[hbm] * 11,
@@ -605,11 +645,12 @@
             pltpu.VMEM((hidden, width), BF16),
             pltpu.VMEM((2, 8, tokens), F32),
             pltpu.VMEM((2, 8, tokens), F32),
-            pltpu.VMEM((2, HEAD, width), BF16),
-            pltpu.VMEM((2, tokens - HEAD, width), BF16),
-            pltpu.VMEM((2, HEAD, width), BF16),
+            pltpu.VMEM((2, HEAD, width - RAW), BF16),
+            pltpu.VMEM((2, tokens - HEAD, width - RAW), BF16),
+            pltpu.VMEM((2, HEAD, width - RAW), BF16),
+            pltpu.VMEM((2, tokens, RAW), BF16),
             pltpu.VMEM((2, 2 * SLOTS, width), BF16),
-            pltpu.VMEM((2, tokens, EXPERTS), BF16),
+            pltpu.VMEM((4, tokens, EXPERTS), BF16),
             pltpu.VMEM((1, EXPERTS), F32),
             pltpu.VMEM((3, EXP_WIN, CAP, width), BF16),
             pltpu.VMEM((3, 2, half, CAP, width), BF16),
@@ -621,7 +662,7 @@
             pltpu.VMEM((SLOTS, width), F32),
             pltpu.VMEM((2, n * CAP, hidden), F32),
             pltpu.VMEM((n, 8, EXPERTS), F32),
-            dma((11,)), dma((5 + PIECES,)), dma((6,)), dma((6,)),
+            dma((11,)), dma((7 + PIECES,)), dma((8,)), dma((8,)),
             dma((3, half)), dma((3, half)), dma((3, half)), dma((3, half)),
             dma((2, PIECES)), dma((2, PIECES)), dma((2, PIECES, half)), dma((2, PIECES, half)),
             dma((n,)), dma((n,)),
@@ -644,10 +685,10 @@
         out_specs=(hbm, hbm, hbm),
         scratch_shapes=[
             pltpu.VMEM((2, rows, width), BF16),
-            pltpu.VMEM((2, tokens, EXPERTS), BF16),
+            pltpu.VMEM((4, tokens, EXPERTS), BF16),
             pltpu.VMEM((1, EXPERTS), F32),
             pltpu.VMEM((2, tokens, width), BF16),
-            dma((width // CHUNK,)), dma((2, width // CHUNK)), dma((3,)),
+            dma((width // RAW,)), dma((2, width // RAW)), dma((3,)),
         ],
         compiler_params=pltpu.CompilerParams(vmem_limit_bytes=60 * 1024 * 1024),
     )(stack, back, balance)

time: 40 us -> 42.8 us (1.070)
  Pallas kernels: 39.1 us -> 42 us
    pallas_call x1, Pallas kernels: 36.5 us -> 39.2 us  [body(): pl.pallas_call(functools.partial(kernel, sections, n), out_shape=(jax.Sha...]
where the time goes in v5:
time: 42.8 us; the launch traced here: 42.6 us
  Pallas kernels  42 us (98%)
  between operations  0.64 us (1%)
    pallas_call x1, Pallas kernels, body(): pl.pallas_call(functools.partial(kernel, sections, n), out_shape=(jax.Sha...  39.2 us
    pallas_call x1, Pallas kernels, body(): pl.pallas_call(place_kernel, out_shape=(jax.ShapeDtypeStruct((tokens, wid...  2.74 us

profile of v5, /device:TPU:0, one launch (start us, length us, event | category | flops | bytes accessed | tf_op | source)
XLA Modules:
  0.0 42.6 jit_solution(12284994143951431431)
XLA Ops:
  0.6 39.2 %shard_map.130 = (bf16[2,96,4096]{2,1,0:T(8,128)(2,1)}, bf16[4,64,128]{2,1,0:T(8,128)(2,1)}, f32[1,128]{1,0:T(1,128)}) custom-call(s32[8,64]{1,0:T(8,128)} %bitcast.24, s32[8,64]{1,0:T(8,128)} %bitcast.25, f32[64,128]{1,0:T(8,128)} %bitcast.22, f32[64,128]{1,0:T(8,128)} %bitcast.23, bf16[64,4096]{1,0:T(8,128)(2,1)} %bitcast.19, bf16[64,4096]{1,0:T(8,128)(2,1)} %bitcast.20, ...), custom_call_target="tpu_custom_call" | custom-call | tf_op jit(solution)/shard_map/pallas_call | solution.py:626
  39.9 2.7 %shard_map.131 = (bf16[64,4096]{1,0:T(8,128)(2,1)}, bf16[64,4096]{1,0:T(8,128)(2,1)}, f32[1,128]{1,0:T(1,128)}) custom-call(bf16[2,96,4096]{2,1,0:T(8,128)(2,1)} %get-tuple-element.9.stack_hbm, bf16[4,64,128]{2,1,0:T(8,128)(2,1)} %get-tuple-element.10.back_hbm, f32[1,128]{1,0:T(1,128)} %get-tuple-element.11.balance_hbm), custom_call_target="tpu_custom_call" | custom-call | tf_op jit(solution)/shard_map/pallas_call | solution.py:677

commit v6 on v4

--- a/solution.py
+++ b/solution.py
@@ -151,7 +151,7 @@
             (wg_hbm, gate_side), (wu_hbm, up_side), (wd_hbm, wd),
         ))
     ]
-    for load in loads:
+    for load in loads[:8]:
         load.start()
 
     barrier = pltpu.get_barrier_semaphore()
@@ -192,16 +192,8 @@
     ]
     for copy in places:
         copy.start()
-
-    loads[2].wait()
-    loads[3].wait()
-    hit, _, f_pick, f_gate, f_back = route_tables(froute_ref[...], flogit_ref[...])
-    _, b_select, b_pick, b_gate, b_back = route_tables(broute_ref[...], blogit_ref[...])
-
-    back_ref[0] = f_back
-    back_ref[1] = b_back
-    back_keep = pltpu.make_async_copy(back_ref, back_hbm, o_sem.at[2])
-    back_keep.start()
+    for load in loads[8:]:
+        load.start()
 
     def peer(d):
         return lax.rem(mine + d, half)
@@ -248,6 +240,8 @@
         for e in range(EXP_WIN):
             slab[kind, e, :, at] = rows[e * CAP : (e + 1) * CAP].astype(BF16)
 
+    loads[3].wait()
+    _, b_select, b_pick, b_gate, b_back = route_tables(broute_ref[...], blogit_ref[...])
     loads[4].wait()
     loads[5].wait()
     sources = (fwd_ref, bwd_ref)
@@ -256,7 +250,7 @@
         places[which].wait_recv()
         orders.append(permutation(place_in[which, 0:1], tokens))
 
-    for which in range(2):
+    for which in (1, 0):
         def fill_head(at, carry, which=which):
             head_out[which, :, at] = dot(orders[which][:HEAD], sources[which][:, at]).astype(BF16)
             return carry
@@ -281,6 +275,13 @@
 
     columns(width, norm_saved, chunk=WIDE)
     dispatch(0)
+
+    loads[2].wait()
+    hit, _, f_pick, f_gate, f_back = route_tables(froute_ref[...], flogit_ref[...])
+    back_ref[0] = f_back
+    back_ref[1] = b_back
+    back_keep = pltpu.make_async_copy(back_ref, back_hbm, o_sem.at[2])
+    back_keep.start()
 
     for which in range(2):
         def fill_tail(at, carry, which=which):
@@ -434,10 +435,10 @@
             for i, d_part in enumerate(d_parts)
         )
 
+    relay(2)
     make_piece(0, 0, input_grad)
     make_piece(0, 1, input_grad)
     give(0, 0)
-    relay(2)
     for p in range(2, PIECES):
         make_piece(0, p, input_grad)
         give(0, p - 1)

time: 40 us -> 42.3 us (1.057)
  Pallas kernels: 39.1 us -> 41.5 us
    pallas_call x1, Pallas kernels: 36.5 us -> 38.8 us  [body(): pl.pallas_call(functools.partial(kernel, sections, n), out_shape=(jax.Sha...]
where the time goes in v6:
time: 42.3 us; the launch traced here: 42.1 us
  Pallas kernels  41.5 us (98%)
  between operations  0.64 us (2%)
    pallas_call x1, Pallas kernels, body(): pl.pallas_call(functools.partial(kernel, sections, n), out_shape=(jax.Sha...  38.8 us
    pallas_call x1, Pallas kernels, body(): pl.pallas_call(place_kernel, out_shape=(jax.ShapeDtypeStruct((tokens, wid...  2.65 us

profile of v6, /device:TPU:0, one launch (start us, length us, event | category | flops | bytes accessed | tf_op | source)
XLA Modules:
  0.0 42.1 jit_solution(12410566463073787026)
XLA Ops:
  0.6 38.8 %shard_map.130 = (bf16[2,96,4096]{2,1,0:T(8,128)(2,1)}, bf16[2,64,128]{2,1,0:T(8,128)(2,1)}, f32[1,128]{1,0:T(1,128)}) custom-call(s32[8,64]{1,0:T(8,128)} %bitcast.24, s32[8,64]{1,0:T(8,128)} %bitcast.25, f32[64,128]{1,0:T(8,128)} %bitcast.22, f32[64,128]{1,0:T(8,128)} %bitcast.23, bf16[64,4096]{1,0:T(8,128)(2,1)} %bitcast.19, bf16[64,4096]{1,0:T(8,128)(2,1)} %bitcast.20, ...), custom_call_target="tpu_custom_call" | custom-call | tf_op jit(solution)/shard_map/pallas_call | solution.py:587
  39.5 2.6 %shard_map.131 = (bf16[64,4096]{1,0:T(8,128)(2,1)}, bf16[64,4096]{1,0:T(8,128)(2,1)}, f32[1,128]{1,0:T(1,128)}) custom-call(bf16[2,96,4096]{2,1,0:T(8,128)(2,1)} %get-tuple-element.9.stack_hbm, bf16[2,64,128]{2,1,0:T(8,128)(2,1)} %get-tuple-element.10.back_hbm, f32[1,128]{1,0:T(1,128)} %get-tuple-element.11.balance_hbm), custom_call_target="tpu_custom_call" | custom-call | tf_op jit(solution)/shard_map/pallas_call | solution.py:637

commit v7 on v6

--- a/solution.py
+++ b/solution.py
@@ -15,7 +15,7 @@
 HEAD = 16
 CHUNK = 1024
 WIDE = 2048
-PIECES = 4
+PIECES = 2
 EPSILON = 1e-06
 MESH = pl.DeviceIdType.MESH
 F32 = jnp.float32

time: 42.3 us -> 41.3 us (0.976)
  Pallas kernels: 41.5 us -> 40.4 us
    pallas_call x1, Pallas kernels: 38.8 us -> 37.8 us  [body(): pl.pallas_call(functools.partial(kernel, sections, n), out_shape=(jax.Sha...]
where the time goes in v7:
time: 41.3 us; the launch traced here: 41.1 us
  Pallas kernels  40.4 us (98%)
  between operations  0.64 us (2%)
    pallas_call x1, Pallas kernels, body(): pl.pallas_call(functools.partial(kernel, sections, n), out_shape=(jax.Sha...  37.8 us
    pallas_call x1, Pallas kernels, body(): pl.pallas_call(place_kernel, out_shape=(jax.ShapeDtypeStruct((tokens, wid...  2.65 us

profile of v7, /device:TPU:0, one launch (start us, length us, event | category | flops | bytes accessed | tf_op | source)
XLA Modules:
  0.0 41.1 jit_solution(17001324712623114657)
XLA Ops:
  0.6 37.8 %shard_map.130 = (bf16[2,96,4096]{2,1,0:T(8,128)(2,1)}, bf16[2,64,128]{2,1,0:T(8,128)(2,1)}, f32[1,128]{1,0:T(1,128)}) custom-call(s32[8,64]{1,0:T(8,128)} %bitcast.24, s32[8,64]{1,0:T(8,128)} %bitcast.25, f32[64,128]{1,0:T(8,128)} %bitcast.22, f32[64,128]{1,0:T(8,128)} %bitcast.23, bf16[64,4096]{1,0:T(8,128)(2,1)} %bitcast.19, bf16[64,4096]{1,0:T(8,128)(2,1)} %bitcast.20, ...), custom_call_target="tpu_custom_call" | custom-call | tf_op jit(solution)/shard_map/pallas_call | solution.py:587
  38.4 2.6 %shard_map.131 = (bf16[64,4096]{1,0:T(8,128)(2,1)}, bf16[64,4096]{1,0:T(8,128)(2,1)}, f32[1,128]{1,0:T(1,128)}) custom-call(bf16[2,96,4096]{2,1,0:T(8,128)(2,1)} %get-tuple-element.9.stack_hbm, bf16[2,64,128]{2,1,0:T(8,128)(2,1)} %get-tuple-element.10.back_hbm, f32[1,128]{1,0:T(1,128)} %get-tuple-element.11.balance_hbm), custom_call_target="tpu_custom_call" | custom-call | tf_op jit(solution)/shard_map/pallas_call | solution.py:637
